TPU v7x, 32 devices: a whole 2x2x4 slice. The times are simulated.
32 devices in a mesh: mod: 2 (over core), seq: 4 (over z), mp: 4 (over y, x).
Axes of the slice: x: 2, y: 2, z: 4, core: 2. Of those that a mesh axis runs over, the one named last changes fastest.
Arguments:
- inputs: bfloat16 [2, 1024, 1024], P('mod', 'seq'), may hold values from -6 to 6
- text_patches: int32 [1024, 4], P('seq'), may hold values from 0 to 255, as said below
- patch_valid: int32 [1024, 4], P('seq'), may hold values 0 or 1
- text_lengths: int32 [4, 2], P('seq'), may hold values from 64 to 192, as said below
- bucket_table: int32 [639], replicated, may hold values from 0 to 31
- attn_gain: bfloat16 [1024], replicated, may hold values from 0.099609375 to 1.8984375
- query_weight: bfloat16 [1024, 1024], P(None, 'mp'), may hold values from -0.1875 to 0.1875
- key_weight: bfloat16 [1024, 1024], P(None, 'mp'), may hold values from -0.1875 to 0.1875
- value_weight: bfloat16 [1024, 1024], P(None, 'mp'), may hold values from -0.1875 to 0.1875
- output_weight: bfloat16 [1024, 1024], P('mp'), may hold values from -1.5 to 1.5
- position_bias: float32 [32, 16], P(None, 'mp'), may hold values from -4 to 4
- ffn_gain: bfloat16 [1024], replicated, may hold values from 0.099609375 to 1.8984375
- gate_weight: bfloat16 [1024, 2816], P(None, 'mp'), may hold values from -0.1875 to 0.1875
- up_weight: bfloat16 [1024, 2816], P(None, 'mp'), may hold values from -0.1875 to 0.1875
- down_weight: bfloat16 [2816, 1024], P('mp'), may hold values from -0.109375 to 0.109375
- cotangent: bfloat16 [2, 1024, 1024], P('mod', 'seq'), may hold values from -6 to 6
Outputs:
- outputs: bfloat16 [2, 1024, 1024], P('mod', 'seq')
- input_grad: float32 [2, 1024, 1024], P('mod', 'seq')
- attn_gain_grad: float32 [1024], P(('mod', 'seq'))
- query_weight_grad: float32 [1024, 1024], P(('mod', 'seq'), 'mp')
- key_weight_grad: float32 [1024, 1024], P(('mod', 'seq'), 'mp')
- value_weight_grad: float32 [1024, 1024], P(('mod', 'seq'), 'mp')
- output_weight_grad: float32 [1024, 1024], P('mp', ('mod', 'seq'))
- position_bias_grad: float32 [32, 16], P(('mod', 'seq'), 'mp')
- ffn_gain_grad: float32 [1024], P(('mod', 'seq'))
- gate_weight_grad: float32 [1024, 2816], P(('mod', 'seq'), 'mp')
- up_weight_grad: float32 [1024, 2816], P(('mod', 'seq'), 'mp')
- down_weight_grad: float32 [2816, 1024], P('mp', ('mod', 'seq'))
Inputs may be any that keep to these rules, and one draw needn't show every extreme that they name: text_patches[t, j] names a patch row of the same seq index inside the text row's own document: from 128 * d to 128 * d + 127 for document d. `text_lengths`: each row holds two lengths, 192 and 64, in either order.
All inputs are finite; a program needn't handle non-finite values. No bound on the sum of `patch_valid` on one device may be relied on, other than what follows from the above.
Results may differ from a plain program's by a relative error of at most 0.015.
Values may be sent and summed in bfloat16 or wider, within the bound.
A program may use at most 128 MiB of HBM per device.

v0:
```python
import math

import jax
import jax.numpy as jnp
from jax import lax
from jax.sharding import PartitionSpec as P

NB = 32
ROWS = 256
PDOC = 128
MAXPOS = 320
SPAN = 639


epsilon = 1e-06
highest = lax.Precision.HIGHEST
root_two_pi = 0.7978845608028654


def shifted(block, axis, distance):
    devices = range(lax.axis_size(axis))
    route = [(i - distance, i) for i in devices if i - distance in devices]
    return lax.ppermute(block, axis, route)


def swapped(value, axis, apart):
    mask = 2**apart
    pairs = [(source, source ^ mask) for source in range(lax.axis_size(axis))]
    return lax.ppermute(value, axis, pairs)


def rms_norm(hidden, gain_values):
    return (
        hidden
        * lax.rsqrt(jnp.mean(hidden * hidden, axis=-1, keepdims=True) + epsilon)
        * gain_values
    )


def gelu_gated(gate_values, up_values):
    cubic = gate_values + 0.044715 * gate_values * gate_values * gate_values
    return 0.5 * gate_values * (1.0 + jnp.tanh(root_two_pi * cubic)) * up_values


def doc_positions(length_row):
    patch_rows = jnp.arange(ROWS, dtype=jnp.int32)
    patch_doc = patch_rows // PDOC
    patch_pos = patch_rows % PDOC
    first_len = length_row[0]
    text_doc = (patch_rows >= first_len).astype(jnp.int32)
    text_pos = PDOC + patch_rows - text_doc * first_len
    return (patch_doc, patch_pos, text_doc, text_pos)


def project(left, right):
    return jnp.dot(left, right, preferred_element_type=jnp.float32)


def per_device(
    inputs,
    text_patches,
    patch_valid,
    text_lengths,
    bucket_table,
    attn_gain,
    query_weight,
    key_weight,
    value_weight,
    output_weight,
    position_bias,
    ffn_gain,
    gate_weight,
    up_weight,
    down_weight,
    cotangent,
):
    low_type = jnp.bfloat16
    own_rows = inputs[0]
    row_count = own_rows.shape[0]
    heads_here = position_bias.shape[1]
    head_dim = query_weight.shape[1] // heads_here
    local_ids = jnp.arange(row_count, dtype=jnp.int32)
    patch_count = jnp.sum(
        (text_patches[:, :, None] == local_ids[None, None, :]).astype(jnp.float32)
        * patch_valid.astype(jnp.float32)[:, :, None],
        axis=1,
    )
    incoming = shifted(own_rows, "mod", 1)
    patch_sum = project(patch_count.astype(low_type), incoming)
    united_rows = own_rows.astype(jnp.float32) + patch_sum
    patch_doc, patch_pos, text_doc, text_pos = doc_positions(text_lengths[0])
    is_text = lax.axis_index("mod") == 1
    own_doc = jnp.where(is_text, text_doc, patch_doc)
    own_pos = jnp.where(is_text, text_pos, patch_pos)
    key_doc = jnp.concatenate([own_doc, jnp.where(is_text, patch_doc, text_doc)])
    key_pos = jnp.concatenate([own_pos, jnp.where(is_text, patch_pos, text_pos)])
    same_doc = own_doc[:, None] == key_doc[None, :]
    pos_ids = jnp.arange(MAXPOS, dtype=jnp.int32)
    own_hot = (own_pos[:, None] == pos_ids[None, :]).astype(jnp.float32)
    key_hot = (key_pos[:, None] == pos_ids[None, :]).astype(jnp.float32)
    bucket_ids = jnp.arange(NB, dtype=jnp.int32)
    table_hot = (bucket_table[:, None] == bucket_ids[None, :]).astype(jnp.float32)
    rel_bias = jnp.dot(table_hot, position_bias, precision=highest)
    pos_block = math.gcd(MAXPOS, 32)
    span_ids = jnp.arange(SPAN, dtype=jnp.int32)
    block_starts = jnp.arange(MAXPOS // pos_block, dtype=jnp.int32) * pos_block

    def diagonal_hot(start):
        first_pos = start + jnp.arange(pos_block, dtype=jnp.int32)
        distance = pos_ids[None, :] - first_pos[:, None] + MAXPOS - 1
        return (distance[:, :, None] == span_ids[None, None, :]).astype(jnp.float32)

    def toeplitz_block(start):
        return jnp.einsum("abs,sh->hab", diagonal_hot(start), rel_bias, precision=highest)

    pos_bias = jnp.moveaxis(lax.map(toeplitz_block, block_starts), 0, 1).reshape(
        heads_here, MAXPOS, MAXPOS
    )
    own_side = jnp.einsum("qa,hab->hqb", own_hot, pos_bias, precision=highest)
    bias_map = jnp.einsum("hqb,kb->hqk", own_side, key_hot, precision=highest)
    attn_gain_f = attn_gain.astype(jnp.float32)
    normed_attn = rms_norm(united_rows, attn_gain_f).astype(low_type)
    queries = project(normed_attn, query_weight).astype(low_type)
    keys_own = project(normed_attn, key_weight).astype(low_type)
    values_own = project(normed_attn, value_weight).astype(low_type)
    keys_other, values_other = swapped((keys_own, values_own), "mod", 0)
    keys_all = jnp.concatenate([keys_own, keys_other], axis=0)
    values_all = jnp.concatenate([values_own, values_other], axis=0)

    def split_heads(matrix):
        return jnp.moveaxis(matrix.reshape(matrix.shape[0], heads_here, head_dim), 1, 0)

    def merge_heads(stacked):
        return jnp.moveaxis(stacked, 0, 1).reshape(stacked.shape[1], heads_here * head_dim)

    head_queries = split_heads(queries)
    head_keys = split_heads(keys_all)
    head_values = split_heads(values_all)

    def head_scores(head_query, head_key, head_bias):
        scores = (
            jnp.einsum("qe,ke->qk", head_query, head_key, preferred_element_type=jnp.float32)
            * 0.125
            + head_bias
        )
        return jnp.where(same_doc, scores, -1000000000.0)

    def forward_head(pieces):
        head_query, head_key, head_value, head_bias = pieces
        scores = head_scores(head_query, head_key, head_bias)
        row_max = jnp.max(scores, axis=-1, keepdims=True)
        unnormed = jnp.exp(scores - row_max)
        row_total = jnp.sum(unnormed, axis=-1, keepdims=True)
        attn_probs = (unnormed / row_total).astype(low_type)
        return (project(attn_probs, head_value), row_max[:, 0], row_total[:, 0])

    head_out, row_maxes, row_totals = lax.map(
        forward_head, (head_queries, head_keys, head_values, bias_map)
    )
    attended = merge_heads(head_out).astype(low_type)
    attn_terms = project(attended, output_weight)
    ffn_gain_f = ffn_gain.astype(jnp.float32)
    middle = united_rows + lax.psum(attn_terms, "mp")
    normed_ffn = rms_norm(middle, ffn_gain_f).astype(low_type)
    gate_values = project(normed_ffn, gate_weight)
    up_values = project(normed_ffn, up_weight)
    hidden = gelu_gated(gate_values, up_values).astype(low_type)
    ffn_terms = project(hidden, down_weight)
    outputs = (middle + lax.psum(ffn_terms.astype(jnp.bfloat16), "mp").astype(jnp.float32)).astype(
        low_type
    )[None]
    tangent_low = cotangent[0]
    tangent = tangent_low.astype(jnp.float32)
    down_weight_grad = jnp.einsum(
        "rf,rd->fd", hidden, tangent_low, preferred_element_type=jnp.float32
    )
    hidden_grad = jnp.einsum(
        "rd,fd->rf", tangent_low, down_weight, preferred_element_type=jnp.float32
    )
    _, gelu_pull = jax.vjp(gelu_gated, gate_values, up_values)
    gate_grad_f, up_grad_f = gelu_pull(hidden_grad)
    gate_low = gate_grad_f.astype(low_type)
    up_low = up_grad_f.astype(low_type)
    gate_weight_grad = jnp.einsum(
        "rd,rf->df", normed_ffn, gate_low, preferred_element_type=jnp.float32
    )
    up_weight_grad = jnp.einsum("rd,rf->df", normed_ffn, up_low, preferred_element_type=jnp.float32)
    ffn_in_part = jnp.einsum(
        "rf,df->rd", gate_low, gate_weight, preferred_element_type=jnp.float32
    ) + jnp.einsum("rf,df->rd", up_low, up_weight, preferred_element_type=jnp.float32)
    ffn_in_grad = lax.psum(ffn_in_part, "mp")
    _, second_pull = jax.vjp(rms_norm, middle, ffn_gain_f)
    middle_norm_grad, ffn_gain_grad = second_pull(ffn_in_grad)
    middle_grad = tangent + middle_norm_grad
    branch_low = middle_grad.astype(low_type)
    output_weight_grad = jnp.einsum(
        "rq,rd->qd", attended, branch_low, preferred_element_type=jnp.float32
    )
    attended_grad = jnp.einsum(
        "rd,qd->rq", branch_low, output_weight, preferred_element_type=jnp.float32
    ).astype(low_type)

    def backward_head(pieces):
        head_query, head_key, head_value, head_bias, head_grad, row_max, row_total = pieces
        scores = head_scores(head_query, head_key, head_bias)
        attn_probs = jnp.exp(scores - row_max[:, None]) / row_total[:, None]
        probs_grad = jnp.einsum(
            "qe,ke->qk", head_grad, head_value, preferred_element_type=jnp.float32
        )
        score_grad = (
            attn_probs * (probs_grad - jnp.sum(attn_probs * probs_grad, axis=-1, keepdims=True))
        ).astype(low_type)
        query_part = (
            jnp.einsum("qk,ke->qe", score_grad, head_key, preferred_element_type=jnp.float32)
            * 0.125
        )
        key_part = (
            jnp.einsum("qk,qe->ke", score_grad, head_query, preferred_element_type=jnp.float32)
            * 0.125
        )
        value_part = jnp.einsum(
            "qk,qe->ke", attn_probs.astype(low_type), head_grad, preferred_element_type=jnp.float32
        )
        key_side = jnp.einsum(
            "qk,kb->qb", score_grad.astype(jnp.float32), key_hot, precision=highest
        )
        pos_grad = jnp.einsum("qa,qb->ab", own_hot, key_side, precision=highest)
        return (query_part, key_part, value_part, pos_grad)

    query_parts, key_parts, value_parts, pos_grads = lax.map(
        backward_head,
        (
            head_queries,
            head_keys,
            head_values,
            bias_map,
            split_heads(attended_grad),
            row_maxes,
            row_totals,
        ),
    )

    def distance_block(pieces):
        start, grad_block = pieces
        return jnp.einsum("abs,hab->sh", diagonal_hot(start), grad_block, precision=highest)

    grad_pos_blocks = jnp.moveaxis(
        pos_grads.reshape(heads_here, MAXPOS // pos_block, pos_block, MAXPOS), 1, 0
    )
    rel_grad = jnp.sum(lax.map(distance_block, (block_starts, grad_pos_blocks)), axis=0)
    position_bias_grad = jnp.einsum("sn,sh->nh", table_hot, rel_grad, precision=highest)
    query_grad_f = merge_heads(query_parts)
    key_grad_all = merge_heads(key_parts)
    value_grad_all = merge_heads(value_parts)
    key_back, value_back = swapped((key_grad_all[row_count:], value_grad_all[row_count:]), "mod", 0)
    query_low = query_grad_f.astype(low_type)
    key_low = (key_grad_all[:row_count] + key_back).astype(low_type)
    value_low = (value_grad_all[:row_count] + value_back).astype(low_type)
    query_weight_grad = jnp.einsum(
        "rd,rq->dq", normed_attn, query_low, preferred_element_type=jnp.float32
    )
    key_weight_grad = jnp.einsum(
        "rd,rq->dq", normed_attn, key_low, preferred_element_type=jnp.float32
    )
    value_weight_grad = jnp.einsum(
        "rd,rq->dq", normed_attn, value_low, preferred_element_type=jnp.float32
    )
    attn_in_part = jnp.einsum(
        "rq,dq->rd", query_low, query_weight, preferred_element_type=jnp.float32
    )
    attn_in_part = attn_in_part + jnp.einsum(
        "rq,dq->rd", key_low, key_weight, preferred_element_type=jnp.float32
    )
    attn_in_part = attn_in_part + jnp.einsum(
        "rq,dq->rd", value_low, value_weight, preferred_element_type=jnp.float32
    )
    attn_in_grad = lax.psum(attn_in_part.astype(jnp.bfloat16), "mp").astype(jnp.float32)
    _, first_pull = jax.vjp(rms_norm, united_rows, attn_gain_f)
    united_norm_grad, attn_gain_grad = first_pull(attn_in_grad)
    united_grad = middle_grad + united_norm_grad
    spread = jnp.einsum("tp,td->pd", patch_count, united_grad, precision=highest)
    returned = shifted(spread.astype(jnp.bfloat16), "mod", -1).astype(spread.dtype)
    input_grad = (united_grad + returned)[None]
    (
        attn_gain_grad,
        query_weight_grad,
        key_weight_grad,
        value_weight_grad,
        output_weight_grad,
        position_bias_grad,
        ffn_gain_grad,
        gate_weight_grad,
        up_weight_grad,
        down_weight_grad,
    ) = (
        lax.psum_scatter(attn_gain_grad, ("mod", "seq"), scatter_dimension=0, tiled=True),
        lax.psum_scatter(query_weight_grad, ("mod", "seq"), scatter_dimension=0, tiled=True),
        lax.psum_scatter(key_weight_grad, ("mod", "seq"), scatter_dimension=0, tiled=True),
        lax.psum_scatter(value_weight_grad, ("mod", "seq"), scatter_dimension=0, tiled=True),
        lax.psum_scatter(output_weight_grad, ("mod", "seq"), scatter_dimension=1, tiled=True),
        lax.psum_scatter(position_bias_grad, ("mod", "seq"), scatter_dimension=0, tiled=True),
        lax.psum_scatter(ffn_gain_grad, ("mod", "seq"), scatter_dimension=0, tiled=True),
        lax.psum_scatter(gate_weight_grad, ("mod", "seq"), scatter_dimension=0, tiled=True),
        lax.psum_scatter(up_weight_grad, ("mod", "seq"), scatter_dimension=0, tiled=True),
        lax.psum_scatter(down_weight_grad, ("mod", "seq"), scatter_dimension=1, tiled=True),
    )
    return (
        outputs,
        input_grad,
        attn_gain_grad,
        query_weight_grad,
        key_weight_grad,
        value_weight_grad,
        output_weight_grad,
        position_bias_grad,
        ffn_gain_grad,
        gate_weight_grad,
        up_weight_grad,
        down_weight_grad,
    )


def solution(mesh):
    in_specs = (
        P("mod", "seq", None),
        P("seq", None),
        P("seq", None),
        P("seq", None),
        P(),
        P(),
        P(None, "mp"),
        P(None, "mp"),
        P(None, "mp"),
        P("mp", None),
        P(None, "mp"),
        P(),
        P(None, "mp"),
        P(None, "mp"),
        P("mp", None),
        P("mod", "seq", None),
    )
    out_specs = (
        P("mod", "seq", None),
        P("mod", "seq", None),
        P(("mod", "seq")),
        P(("mod", "seq"), "mp"),
        P(("mod", "seq"), "mp"),
        P(("mod", "seq"), "mp"),
        P("mp", ("mod", "seq")),
        P(("mod", "seq"), "mp"),
        P(("mod", "seq")),
        P(("mod", "seq"), "mp"),
        P(("mod", "seq"), "mp"),
        P("mp", ("mod", "seq")),
    )
    return jax.shard_map(
        per_device, mesh=mesh, in_specs=in_specs, out_specs=out_specs, check_vma=False
    )
```

profile of v0, /device:TPU:0, one launch (start us, length us, event | category | flops | bytes accessed | tf_op | source)
XLA Modules:
  0.0 833.9 jit_solution(8737926940876682966)
XLA Ops:
  14.9 161.8 %while.62 = (s32[]{:T(128)}, f32[10,4,32,320]{3,1,2,0:T(4,128)S(1)}, s32[10]{0:T(128)}, f32[639,4]{0,1:T(4,128)S(1)}, s32[]{:T(128)}) while((s32[]{:T(128)}, f32[10,4,32,320]{3,1,2,0:T(4,128)S(1)}, s32[10]{0:T(128)}, f32[639,4]{0,1:T(4,128)S(1)}, s32[]{:T(128)}) %tuple.130), condition=%wide.region_3.4_spmd.clone, body=%wide.region_2.3_spmd.clone.sunk | while | flops 320645152 | bytes 297297 | solution.py:116
  16.9 14.2 %fusion.214 = f32[10,4,32,320]{3,1,2,0:T(4,128)S(1)} fusion(f32[10,4,32,320]{3,1,2,0:T(4,128)S(1)} %get-tuple-element.882, s32[]{:T(128)} %get-tuple-element.881, s32[32,320]{1,0:T(8,128)S(1)} %fusion.213, f32[639,4]{0,1:T(4,128)S(1)} %get-tuple-element.889), kind=kOutput, calls=%fused_computation.12.clone.1 | convolution fusion | flops 320624640 | bytes 256004 | tf_op jit(solution)/shard_map/while/body/eval_jaxpr/abs,sh->hab/dot_general | solution.py:114
  33.1 14.2 %fusion.214 = f32[10,4,32,320]{3,1,2,0:T(4,128)S(1)} fusion(f32[10,4,32,320]{3,1,2,0:T(4,128)S(1)} %get-tuple-element.882, s32[]{:T(128)} %get-tuple-element.881, s32[32,320]{1,0:T(8,128)S(1)} %fusion.213, f32[639,4]{0,1:T(4,128)S(1)} %get-tuple-element.889), kind=kOutput, calls=%fused_computation.12.clone.1 | convolution fusion | flops 320624640 | bytes 256004 | tf_op jit(solution)/shard_map/while/body/eval_jaxpr/abs,sh->hab/dot_general | solution.py:114
  49.3 14.2 %fusion.214 = f32[10,4,32,320]{3,1,2,0:T(4,128)S(1)} fusion(f32[10,4,32,320]{3,1,2,0:T(4,128)S(1)} %get-tuple-element.882, s32[]{:T(128)} %get-tuple-element.881, s32[32,320]{1,0:T(8,128)S(1)} %fusion.213, f32[639,4]{0,1:T(4,128)S(1)} %get-tuple-element.889), kind=kOutput, calls=%fused_computation.12.clone.1 | convolution fusion | flops 320624640 | bytes 256004 | tf_op jit(solution)/shard_map/while/body/eval_jaxpr/abs,sh->hab/dot_general | solution.py:114
  65.5 14.2 %fusion.214 = f32[10,4,32,320]{3,1,2,0:T(4,128)S(1)} fusion(f32[10,4,32,320]{3,1,2,0:T(4,128)S(1)} %get-tuple-element.882, s32[]{:T(128)} %get-tuple-element.881, s32[32,320]{1,0:T(8,128)S(1)} %fusion.213, f32[639,4]{0,1:T(4,128)S(1)} %get-tuple-element.889), kind=kOutput, calls=%fused_computation.12.clone.1 | convolution fusion | flops 320624640 | bytes 256004 | tf_op jit(solution)/shard_map/while/body/eval_jaxpr/abs,sh->hab/dot_general | solution.py:114
  81.7 14.2 %fusion.214 = f32[10,4,32,320]{3,1,2,0:T(4,128)S(1)} fusion(f32[10,4,32,320]{3,1,2,0:T(4,128)S(1)} %get-tuple-element.882, s32[]{:T(128)} %get-tuple-element.881, s32[32,320]{1,0:T(8,128)S(1)} %fusion.213, f32[639,4]{0,1:T(4,128)S(1)} %get-tuple-element.889), kind=kOutput, calls=%fused_computation.12.clone.1 | convolution fusion | flops 320624640 | bytes 256004 | tf_op jit(solution)/shard_map/while/body/eval_jaxpr/abs,sh->hab/dot_general | solution.py:114
  97.8 14.2 %fusion.214 = f32[10,4,32,320]{3,1,2,0:T(4,128)S(1)} fusion(f32[10,4,32,320]{3,1,2,0:T(4,128)S(1)} %get-tuple-element.882, s32[]{:T(128)} %get-tuple-element.881, s32[32,320]{1,0:T(8,128)S(1)} %fusion.213, f32[639,4]{0,1:T(4,128)S(1)} %get-tuple-element.889), kind=kOutput, calls=%fused_computation.12.clone.1 | convolution fusion | flops 320624640 | bytes 256004 | tf_op jit(solution)/shard_map/while/body/eval_jaxpr/abs,sh->hab/dot_general | solution.py:114
  114.0 14.2 %fusion.214 = f32[10,4,32,320]{3,1,2,0:T(4,128)S(1)} fusion(f32[10,4,32,320]{3,1,2,0:T(4,128)S(1)} %get-tuple-element.882, s32[]{:T(128)} %get-tuple-element.881, s32[32,320]{1,0:T(8,128)S(1)} %fusion.213, f32[639,4]{0,1:T(4,128)S(1)} %get-tuple-element.889), kind=kOutput, calls=%fused_computation.12.clone.1 | convolution fusion | flops 320624640 | bytes 256004 | tf_op jit(solution)/shard_map/while/body/eval_jaxpr/abs,sh->hab/dot_general | solution.py:114
  130.2 14.2 %fusion.214 = f32[10,4,32,320]{3,1,2,0:T(4,128)S(1)} fusion(f32[10,4,32,320]{3,1,2,0:T(4,128)S(1)} %get-tuple-element.882, s32[]{:T(128)} %get-tuple-element.881, s32[32,320]{1,0:T(8,128)S(1)} %fusion.213, f32[639,4]{0,1:T(4,128)S(1)} %get-tuple-element.889), kind=kOutput, calls=%fused_computation.12.clone.1 | convolution fusion | flops 320624640 | bytes 256004 | tf_op jit(solution)/shard_map/while/body/eval_jaxpr/abs,sh->hab/dot_general | solution.py:114
  146.4 14.2 %fusion.214 = f32[10,4,32,320]{3,1,2,0:T(4,128)S(1)} fusion(f32[10,4,32,320]{3,1,2,0:T(4,128)S(1)} %get-tuple-element.882, s32[]{:T(128)} %get-tuple-element.881, s32[32,320]{1,0:T(8,128)S(1)} %fusion.213, f32[639,4]{0,1:T(4,128)S(1)} %get-tuple-element.889), kind=kOutput, calls=%fused_computation.12.clone.1 | convolution fusion | flops 320624640 | bytes 256004 | tf_op jit(solution)/shard_map/while/body/eval_jaxpr/abs,sh->hab/dot_general | solution.py:114
  162.6 14.2 %fusion.214 = f32[10,4,32,320]{3,1,2,0:T(4,128)S(1)} fusion(f32[10,4,32,320]{3,1,2,0:T(4,128)S(1)} %get-tuple-element.882, s32[]{:T(128)} %get-tuple-element.881, s32[32,320]{1,0:T(8,128)S(1)} %fusion.213, f32[639,4]{0,1:T(4,128)S(1)} %get-tuple-element.889), kind=kOutput, calls=%fused_computation.12.clone.1 | convolution fusion | flops 320624640 | bytes 256004 | tf_op jit(solution)/shard_map/while/body/eval_jaxpr/abs,sh->hab/dot_general | solution.py:114
  189.8 21.8 %while.63 = (s32[]{:T(128)}, bf16[4,256,64]{1,2,0:T(8,128)(2,1)S(1)}, f32[4,256]{1,0:T(4,128)}, f32[4,256]{1,0:T(4,128)}, bf16[4,256,64]{2,1,0:T(8,128)(2,1)S(1)...) while((s32[]{:T(128)}, ...), condition=%wide.region_7.8_spmd.clone, body=%wide.region_4.7_spmd.clone.sunk | while | flops 34864640 | bytes 2505341 | solution.py:157
  213.7 54.0 %all-reduce.9.cloned.1.call-done = f32[256,1024]{1,0:T(8,128)} async-done(((f32[256,1024]{1,0:T(8,128)}), f32[256,1024]{1,0:T(8,128)}) %all-reduce.9.cloned.1.call-update) | async-done | bytes 1048592 | tf_op jit(solution)/shard_map/psum | solution.py:163
  279.0 50.2 %all-reduce.11.cloned.1.call-done = f32[256,1024]{1,0:T(8,128)} async-done(((f32[256,1024]{1,0:T(8,128)}), f32[256,1024]{1,0:T(8,128)}) %all-reduce.11.cloned.1.call-update) | async-done | bytes 1048592 | tf_op jit(solution)/shard_map/psum | solution.py:191
  334.5 84.7 %while.64 = (s32[]{:T(128)}, bf16[4,256,64]{1,2,0:T(8,128)(2,1)}, f32[4,512,64]{1,2,0:T(8,128)}, f32[4,512,64]{1,2,0:T(8,128)}, f32[4,320,320]{2,0,1:T(4,128)}, ...) while((s32[]{:T(128)}, bf16[4,256,64]{1,2,0:T(8,128)(2,1)}, ...), condition=%wide.region_15.16_spmd.clone, body=%wide.region_13.15_spmd.clone.sunk | while | flops 903888640 | bytes 9473765 | solution.py:230
  340.4 11.0 %dynamic_update_slice.76 = f32[4,320,320]{2,0,1:T(4,128)} dynamic-update-slice(f32[4,320,320]{2,0,1:T(4,128)} %get-tuple-element.949, f32[1,320,320]{2,0,1:T(1,128)S(1)} %copy.83, s32[]{:T(128)} %get-tuple-element.945, s32[]{:T(128)} %constant.185.clone.1..sunk.1, s32[]{:T(128)} %constant.185.clone.1..sunk.1) | dynamic-update-slice | bytes 819204 | tf_op jit(solution)/shard_map/while/body/jit(dynamic_update_index_in_dim)/dynamic_update_slice | solution.py:230
  361.6 11.0 %dynamic_update_slice.76 = f32[4,320,320]{2,0,1:T(4,128)} dynamic-update-slice(f32[4,320,320]{2,0,1:T(4,128)} %get-tuple-element.949, f32[1,320,320]{2,0,1:T(1,128)S(1)} %copy.83, s32[]{:T(128)} %get-tuple-element.945, s32[]{:T(128)} %constant.185.clone.1..sunk.1, s32[]{:T(128)} %constant.185.clone.1..sunk.1) | dynamic-update-slice | bytes 819204 | tf_op jit(solution)/shard_map/while/body/jit(dynamic_update_index_in_dim)/dynamic_update_slice | solution.py:230
  382.8 11.0 %dynamic_update_slice.76 = f32[4,320,320]{2,0,1:T(4,128)} dynamic-update-slice(f32[4,320,320]{2,0,1:T(4,128)} %get-tuple-element.949, f32[1,320,320]{2,0,1:T(1,128)S(1)} %copy.83, s32[]{:T(128)} %get-tuple-element.945, s32[]{:T(128)} %constant.185.clone.1..sunk.1, s32[]{:T(128)} %constant.185.clone.1..sunk.1) | dynamic-update-slice | bytes 819204 | tf_op jit(solution)/shard_map/while/body/jit(dynamic_update_index_in_dim)/dynamic_update_slice | solution.py:230
  404.0 11.0 %dynamic_update_slice.76 = f32[4,320,320]{2,0,1:T(4,128)} dynamic-update-slice(f32[4,320,320]{2,0,1:T(4,128)} %get-tuple-element.949, f32[1,320,320]{2,0,1:T(1,128)S(1)} %copy.83, s32[]{:T(128)} %get-tuple-element.945, s32[]{:T(128)} %constant.185.clone.1..sunk.1, s32[]{:T(128)} %constant.185.clone.1..sunk.1) | dynamic-update-slice | bytes 819204 | tf_op jit(solution)/shard_map/while/body/jit(dynamic_update_index_in_dim)/dynamic_update_slice | solution.py:230
  443.2 116.4 %while.65 = (s32[]{:T(128)}, f32[10,639,4]{1,2,0:T(4,128)}, s32[10]{0:T(128)}, f32[10,4,32,320]{3,1,2,0:T(4,128)}, s32[]{:T(128)}) while((s32[]{:T(128)}, f32[10,639,4]{1,2,0:T(4,128)}, s32[10]{0:T(128)}, f32[10,4,32,320]{3,1,2,0:T(4,128)}, s32[]{:T(128)}) %tuple.169), condition=%wide.region_25.26_spmd.clone, body=%wide.region_24.25_spmd.clone.sunk | while | flops 320645152 | bytes 290125 | solution.py:250
  445.3 9.6 %fusion.238 = f32[10,639,4]{1,2,0:T(4,128)} fusion(f32[10,639,4]{1,2,0:T(4,128)} %get-tuple-element.987, s32[]{:T(128)} %get-tuple-element.986, s32[32,320]{1,0:T(8,128)S(1)} %fusion.237, f32[10,4,32,320]{3,1,2,0:T(4,128)} %get-tuple-element.994), kind=kOutput, calls=%fused_computation.84.clone.1 | convolution fusion | flops 320624640 | bytes 248832 | tf_op jit(solution)/shard_map/while/body/eval_jaxpr/abs,hab->sh/dot_general | solution.py:245
  456.9 9.6 %fusion.238 = f32[10,639,4]{1,2,0:T(4,128)} fusion(f32[10,639,4]{1,2,0:T(4,128)} %get-tuple-element.987, s32[]{:T(128)} %get-tuple-element.986, s32[32,320]{1,0:T(8,128)S(1)} %fusion.237, f32[10,4,32,320]{3,1,2,0:T(4,128)} %get-tuple-element.994), kind=kOutput, calls=%fused_computation.84.clone.1 | convolution fusion | flops 320624640 | bytes 248832 | tf_op jit(solution)/shard_map/while/body/eval_jaxpr/abs,hab->sh/dot_general | solution.py:245
  468.6 9.6 %fusion.238 = f32[10,639,4]{1,2,0:T(4,128)} fusion(f32[10,639,4]{1,2,0:T(4,128)} %get-tuple-element.987, s32[]{:T(128)} %get-tuple-element.986, s32[32,320]{1,0:T(8,128)S(1)} %fusion.237, f32[10,4,32,320]{3,1,2,0:T(4,128)} %get-tuple-element.994), kind=kOutput, calls=%fused_computation.84.clone.1 | convolution fusion | flops 320624640 | bytes 248832 | tf_op jit(solution)/shard_map/while/body/eval_jaxpr/abs,hab->sh/dot_general | solution.py:245
  480.2 9.6 %fusion.238 = f32[10,639,4]{1,2,0:T(4,128)} fusion(f32[10,639,4]{1,2,0:T(4,128)} %get-tuple-element.987, s32[]{:T(128)} %get-tuple-element.986, s32[32,320]{1,0:T(8,128)S(1)} %fusion.237, f32[10,4,32,320]{3,1,2,0:T(4,128)} %get-tuple-element.994), kind=kOutput, calls=%fused_computation.84.clone.1 | convolution fusion | flops 320624640 | bytes 248832 | tf_op jit(solution)/shard_map/while/body/eval_jaxpr/abs,hab->sh/dot_general | solution.py:245
  503.5 9.6 %fusion.238 = f32[10,639,4]{1,2,0:T(4,128)} fusion(f32[10,639,4]{1,2,0:T(4,128)} %get-tuple-element.987, s32[]{:T(128)} %get-tuple-element.986, s32[32,320]{1,0:T(8,128)S(1)} %fusion.237, f32[10,4,32,320]{3,1,2,0:T(4,128)} %get-tuple-element.994), kind=kOutput, calls=%fused_computation.84.clone.1 | convolution fusion | flops 320624640 | bytes 248832 | tf_op jit(solution)/shard_map/while/body/eval_jaxpr/abs,hab->sh/dot_general | solution.py:245
  515.1 9.6 %fusion.238 = f32[10,639,4]{1,2,0:T(4,128)} fusion(f32[10,639,4]{1,2,0:T(4,128)} %get-tuple-element.987, s32[]{:T(128)} %get-tuple-element.986, s32[32,320]{1,0:T(8,128)S(1)} %fusion.237, f32[10,4,32,320]{3,1,2,0:T(4,128)} %get-tuple-element.994), kind=kOutput, calls=%fused_computation.84.clone.1 | convolution fusion | flops 320624640 | bytes 248832 | tf_op jit(solution)/shard_map/while/body/eval_jaxpr/abs,hab->sh/dot_general | solution.py:245
  550.0 9.6 %fusion.238 = f32[10,639,4]{1,2,0:T(4,128)} fusion(f32[10,639,4]{1,2,0:T(4,128)} %get-tuple-element.987, s32[]{:T(128)} %get-tuple-element.986, s32[32,320]{1,0:T(8,128)S(1)} %fusion.237, f32[10,4,32,320]{3,1,2,0:T(4,128)} %get-tuple-element.994), kind=kOutput, calls=%fused_computation.84.clone.1 | convolution fusion | flops 320624640 | bytes 248832 | tf_op jit(solution)/shard_map/while/body/eval_jaxpr/abs,hab->sh/dot_general | solution.py:245
  568.9 31.7 %all-reduce.3 = (f32[1024]{0:T(1024)}, f32[32,4]{1,0:T(8,128)}, f32[1024]{0:T(1024)}) all-reduce(f32[1024]{0:T(1024)S(1)} %get-tuple-element.560, f32[32,4]{1,0:T(8,128)} %fusion.115, f32[1024]{0:T(1024)S(1)} %copy-done.44), channel_id=2, replica_groups=mesh['mod'=2,'seq'=4,'mp'=4] {'mod','seq'}, use_global_device_ids=true, to_apply=%region_19.20.clone | all-reduce | flops 2176 | bytes 17408
  609.1 20.4 %reduce-scatter.10.cloned.1.call-done = f32[128,256]{1,0:T(8,128)} async-done(((f32[1024,256]{1,0:T(8,128)}), f32[128,256]{1,0:T(8,128)}) %reduce-scatter.10.cloned.1.call-update) | async-done | bytes 131088 | tf_op jit(solution)/shard_map/reduce_scatter | solution.py:298
  629.6 65.7 %reduce-scatter.16.cloned.1.call-done = f32[128,704]{0,1:T(8,128)} async-done(((f32[1024,704]{0,1:T(8,128)}), f32[128,704]{0,1:T(8,128)}) %reduce-scatter.16.cloned.1.call-update) | async-done | bytes 360464 | tf_op jit(solution)/shard_map/reduce_scatter | solution.py:303
  695.3 66.0 %reduce-scatter.18.cloned.1.call-done = f32[128,704]{0,1:T(8,128)} async-done(((f32[1024,704]{0,1:T(8,128)}), f32[128,704]{0,1:T(8,128)}) %reduce-scatter.18.cloned.1.call-update) | async-done | bytes 360464 | tf_op jit(solution)/shard_map/reduce_scatter | solution.py:304
  761.2 65.8 %reduce-scatter.20.cloned.1.call-done = f32[704,128]{1,0:T(8,128)} async-done(((f32[704,1024]{1,0:T(8,128)}), f32[704,128]{1,0:T(8,128)}) %reduce-scatter.20.cloned.1.call-update) | async-done | bytes 360464 | tf_op jit(solution)/shard_map/reduce_scatter | solution.py:305
  (355 shorter events, 210.5 us)
Async XLA Ops:
  7.2 264.6 %copy-start = (bf16[704,1024]{1,0:T(8,128)(2,1)S(1)}, bf16[704,1024]{1,0:T(8,128)(2,1)}, u32[]{:S(2)}) copy-start(bf16[704,1024]{1,0:T(8,128)(2,1)} %param.38) | copy-start | bytes 4325380
  7.2 260.5 %all-reduce.9.cloned.1.call-start = ((), (), s32[]{:S(2)}) async-start(), calls=%async_computation.7 | async-start | bytes 2097152 | tf_op jit(solution)/shard_map/psum | solution.py:163
  7.2 175.1 %collective-permute-start = (bf16[256,1024]{1,0:T(8,128)(2,1)}, bf16[256,1024]{1,0:T(8,128)(2,1)}, u32[]{:S(2)}, u32[]{:S(2)}) collective-permute-start(bf16[256,1024]{1,0:T(8,128)(2,1)} %bitcast.257), channel_id=1, source_target_pairs={{0,16},{1,17},{2,18},{3,19},{4,20},{5,21},{6,22},{7,23},{8,24},{9,... | collective-permute-start | bytes 1572872 | tf_op jit(solution)/shard_map/ppermute | solution.py:23
  12.5 166.3 %copy-start.40 = (s32[256]{0:T(256)}, s32[256]{0:T(256)S(1)}, u32[]{:S(2)}) copy-start(s32[256]{0:T(256)S(1)} %get-tuple-element.940) | copy-start | bytes 3076
  183.8 83.8 %copy-start.1 = (f32[256,1024]{1,0:T(8,128)}, f32[256,1024]{1,0:T(8,128)S(1)}, u32[]{:S(2)}) copy-start(f32[256,1024]{1,0:T(8,128)S(1)} %get-tuple-element.651) | copy-start | bytes 3145732
  184.9 1.5 collective-permute-start.2
  185.6 3.0 collective-permute-start.1
  189.7 21.8 %copy-start.19 = (bf16[256,1024]{1,0:T(8,128)(2,1)S(1)}, bf16[256,1024]{1,0:T(8,128)(2,1)}, u32[]{:S(2)}) copy-start(bf16[256,1024]{1,0:T(8,128)(2,1)} %param.33) | copy-start | bytes 1572868
  212.9 116.3 %all-reduce.11.cloned.1.call-start = ((), (), s32[]{:S(2)}) async-start(), calls=%async_computation.8 | async-start | bytes 2097152 | tf_op jit(solution)/shard_map/psum | solution.py:191
  269.2 62.1 %copy-start.5 = (f32[256,1024]{1,0:T(8,128)}, f32[256,1024]{1,0:T(8,128)S(1)}, u32[]{:S(2)}) copy-start(f32[256,1024]{1,0:T(8,128)S(1)} %get-tuple-element.636) | copy-start | bytes 3145732
  276.4 52.7 %copy-start.39 = (f32[1024]{0:T(1024)S(1)}, f32[1024]{0:T(1024)}, u32[]{:S(2)}) copy-start(f32[1024]{0:T(1024)} %convert_element_type.132) | copy-start | bytes 12292
  276.5 284.7 %all-reduce.13.cloned.1.call-start = ((), (), s32[]{:S(2)}) async-start(), calls=%async_computation.16 | async-start | bytes 2097152 | tf_op jit(solution)/shard_map/psum | solution.py:169
  276.6 54.8 %copy-start.50 = (f32[256]{0:T(256)S(1)}, f32[256]{0:T(256)}, u32[]{:S(2)}) copy-start(f32[256]{0:T(256)} %copy-done.49) | copy-start | bytes 3076
  340.4 13.5 %copy-start.32 = (bf16[4,256,64]{1,2,0:T(8,128)(2,1)S(1)}, bf16[4,256,64]{1,2,0:T(8,128)(2,1)}, u32[]{:S(2)}) copy-start(bf16[4,256,64]{1,2,0:T(8,128)(2,1)} %get-tuple-element.946) | copy-start | bytes 393220 | tf_op jit(solution)/shard_map/while
  361.6 13.5 %copy-start.32 = (bf16[4,256,64]{1,2,0:T(8,128)(2,1)S(1)}, bf16[4,256,64]{1,2,0:T(8,128)(2,1)}, u32[]{:S(2)}) copy-start(bf16[4,256,64]{1,2,0:T(8,128)(2,1)} %get-tuple-element.946) | copy-start | bytes 393220 | tf_op jit(solution)/shard_map/while
  382.8 13.5 %copy-start.32 = (bf16[4,256,64]{1,2,0:T(8,128)(2,1)S(1)}, bf16[4,256,64]{1,2,0:T(8,128)(2,1)}, u32[]{:S(2)}) copy-start(bf16[4,256,64]{1,2,0:T(8,128)(2,1)} %get-tuple-element.946) | copy-start | bytes 393220 | tf_op jit(solution)/shard_map/while
  403.9 13.5 %copy-start.32 = (bf16[4,256,64]{1,2,0:T(8,128)(2,1)S(1)}, bf16[4,256,64]{1,2,0:T(8,128)(2,1)}, u32[]{:S(2)}) copy-start(bf16[4,256,64]{1,2,0:T(8,128)(2,1)} %get-tuple-element.946) | copy-start | bytes 393220 | tf_op jit(solution)/shard_map/while
  420.4 3.3 collective-permute-start.4
  421.6 1.7 collective-permute-start.3
  425.6 183.6 %reduce-scatter.14.cloned.1.call-start = ((), (), s32[]{:S(2)}) async-start(), calls=%async_computation.12 | async-start | bytes 1179648 | tf_op jit(solution)/shard_map/reduce_scatter | solution.py:300
  427.0 182.1 %reduce-scatter.8.cloned.1.call-start = ((), (), s32[]{:S(2)}) async-start(), calls=%async_computation.9 | async-start | bytes 1179648 | tf_op jit(solution)/shard_map/reduce_scatter | solution.py:297
  428.4 180.7 %reduce-scatter.12.cloned.1.call-start = ((), (), s32[]{:S(2)}) async-start(), calls=%async_computation.11 | async-start | bytes 1179648 | tf_op jit(solution)/shard_map/reduce_scatter | solution.py:299
  429.8 199.7 %reduce-scatter.10.cloned.1.call-start = ((), (), s32[]{:S(2)}) async-start(), calls=%async_computation.10 | async-start | bytes 1179648 | tf_op jit(solution)/shard_map/reduce_scatter | solution.py:298
  432.2 263.1 %reduce-scatter.16.cloned.1.call-start = ((), (), s32[]{:S(2)}) async-start(), calls=%async_computation.13 | async-start | bytes 3244032 | tf_op jit(solution)/shard_map/reduce_scatter | solution.py:303
  435.4 325.9 %reduce-scatter.18.cloned.1.call-start = ((), (), s32[]{:S(2)}) async-start(), calls=%async_computation.14 | async-start | bytes 3244032 | tf_op jit(solution)/shard_map/reduce_scatter | solution.py:304
  438.5 388.6 %reduce-scatter.20.cloned.1.call-start = ((), (), s32[]{:S(2)}) async-start(), calls=%async_computation.15 | async-start | bytes 3244032 | tf_op jit(solution)/shard_map/reduce_scatter | solution.py:305
  443.2 118.0 %copy-start.2 = (f32[256,1024]{1,0:T(8,128)S(1)}, f32[256,1024]{1,0:T(8,128)}, u32[]{:S(2)}) copy-start(f32[256,1024]{1,0:T(8,128)} %copy-done.1) | copy-start | bytes 3145732
  443.2 118.0 %copy-start.43 = (f32[256]{0:T(256)S(1)}, f32[256]{0:T(256)}, u32[]{:S(2)}) copy-start(f32[256]{0:T(256)} %copy-done.42) | copy-start | bytes 3076
  562.6 6.3 copy-start.44
  566.5 40.2 %collective-permute-start.5 = (bf16[256,1024]{1,0:T(8,128)(2,1)}, bf16[256,1024]{1,0:T(8,128)(2,1)}, u32[]{:S(2)}, u32[]{:S(2)}) collective-permute-start(bf16[256,1024]{1,0:T(8,128)(2,1)} %convolution_convert_fusion), channel_id=1, source_target_pairs={{16,0},{17,1},{18,2},{19,3},{20,4},{21,5},{22,6},{23,7},{24,8},{25... | collective-permute-start | bytes 1572872 | tf_op jit(solution)/shard_map/ppermute | solution.py:23
  600.6 6.2 copy-start.12
  600.6 6.2 copy-start.47
  (45 other events, 86.8 us)
Sparse Core Ops, SparseCore 0:
  213.0 54.6 all-reduce.8
  276.6 52.5 all-reduce.10
  425.7 52.7 all-reduce.12
  481.2 35.6 reduce-scatter.13
  519.5 34.6 reduce-scatter.7
  557.0 34.5 reduce-scatter.11
  594.5 35.0 reduce-scatter.9
  632.5 62.7 reduce-scatter.15
  698.1 63.0 reduce-scatter.17
  764.0 63.0 reduce-scatter.19
where the time goes:
time: 838 us; the launch traced here: 834 us
  waiting for transfers between devices  323 us (39%)
  matrix products  318 us (38%)
  local copies, waits for them, and re-layouts  105 us (13%)
  other arithmetic  33.7 us (4%)
  blocking collectives  31.7 us (4%)
  between operations  16.1 us (2%)
    dot_general x10, matrix products, toeplitz_block(): jnp.einsum('abs,sh->hab', diagonal_hot(start), rel_bias, precision=highest)  142 us
    dot_general x10, matrix products, distance_block(): jnp.einsum('abs,hab->sh', diagonal_hot(start), grad_block, precision=high...  96.4 us
    reduce_scatter x1, waiting for transfers between devices, per_device(): lax.psum_scatter(up_weight_grad, ('mod', 'seq'), scatter_dimension=0, til...  66 us
    reduce_scatter x1, waiting for transfers between devices, per_device(): lax.psum_scatter(down_weight_grad, ('mod', 'seq'), scatter_dimension=1, t...  65.8 us
    reduce_scatter x1, waiting for transfers between devices, per_device(): lax.psum_scatter(gate_weight_grad, ('mod', 'seq'), scatter_dimension=0, t...  65.7 us
    psum x1, waiting for transfers between devices, per_device(): middle = united_rows + lax.psum(attn_terms, 'mp')  54 us
    psum x1, waiting for transfers between devices, per_device(): ffn_in_grad = lax.psum(ffn_in_part, 'mp')  50.2 us
    dynamic_update_slice x8, local copies, waits for them, and re-layouts, per_device(): lax.map(backward_head, (head_queries, head_keys, head_values, bias_map, s...  47.2 us
  transfers between devices with their start and end apart: 16, of which 7 were waited for; matrix products, arithmetic and copies ran while one was open for 39% of the time, Pallas kernels for 0%

commit v1 on v0

v1 whole, which is shorter than its diff:
```python
import functools
import types

import jax
import jax.numpy as jnp
from jax import lax
from jax.experimental import pallas as pl
from jax.experimental.pallas import tpu as pltpu
from jax.sharding import PartitionSpec as P

MESH = pl.DeviceIdType.MESH
EPS = 1e-06
ROOT = 0.7978845608028654
HEAD = 64
NB = 32
PDOC = 128
LONG = 192
SPANS = 640
WIDE = 896
f32 = jnp.float32
bf16 = jnp.bfloat16


def nn(a, b):
    return jnp.dot(a, b, preferred_element_type=f32)


def nt(a, b):
    return lax.dot_general(a, b, (((1,), (1,)), ((), ())), preferred_element_type=f32)


def rms_scale(x):
    return lax.rsqrt(jnp.mean(x * x, axis=-1, keepdims=True) + EPS)


def row_chunks(total, step, body):
    def one(i, carry):
        body(pl.ds(pl.multiple_of(i * step, step), step))
        return carry

    lax.fori_loop(0, total // step, one, 0)


def bucket_hot(ids_row):
    return (lax.broadcasted_iota(jnp.int32, (NB, SPANS), 0) == ids_row).astype(f32)


def patch_counts(ids, valid, rows):
    places = lax.broadcasted_iota(jnp.int32, (rows, rows), 0)
    count = jnp.zeros((rows, rows), f32)
    for j in range(ids.shape[0]):
        count += jnp.where(ids[j : j + 1, :] == places, valid[j : j + 1, :].astype(f32), 0.0)
    return count


def flat(ref):
    value = ref[...].astype(f32)
    return jnp.concatenate([value[i : i + 1, :] for i in range(value.shape[0])], axis=1)


def sizes_of(heads, ff):
    width = heads * HEAD
    return (ff, ff, ff, width, 3 * width)


def mega(n_seq, n_mp, heads, order, *refs):
    ref, refs = types.SimpleNamespace(), list(refs)
    for name, many in order:
        setattr(ref, name, [refs.pop(0) for _ in range(many)] if many else refs.pop(0))
    mod, seq, mp = lax.axis_index("mod"), lax.axis_index("seq"), lax.axis_index("mp")
    rows, dim = ref.united.shape
    width = heads * HEAD
    ff = ref.wg.shape[0]
    half = dim // 2
    block = half // n_seq
    own_rows = rows // n_mp
    mine = pl.ds(pl.multiple_of(mp * own_rows, own_rows), own_rows)
    here = pl.ds(pl.multiple_of(mod * half, half), half)
    there = pl.ds(pl.multiple_of((1 - mod) * half, half), half)
    sibling = (1 - mod, seq, mp)
    used = [0]
    sends = []

    def peer_of(o):
        if n_mp == 4:
            return (mp + 1 - 2 * (mp % 2), (mp + 2) % 4, 3 - mp)[o - 1]
        return (mp + o) % n_mp

    def source_of(o):
        if n_mp == 4:
            return peer_of(o)
        return (mp + n_mp - o) % n_mp

    def message(src, dst, device, cond=None):
        index = used[0]
        used[0] += 1
        copy = pltpu.make_async_remote_copy(
            src_ref=src,
            dst_ref=dst,
            send_sem=ref.ssem.at[index],
            recv_sem=ref.rsem.at[index],
            device_id=device,
            device_id_type=MESH,
        )
        sends.append((cond, copy))
        return copy

    loads = types.SimpleNamespace()
    pairs = (
        (ref.inp_h.at[0], ref.inp), (ref.ids_h, ref.ids), (ref.pb_h, ref.pb), (ref.tp_h, ref.tp), (ref.pv_h, ref.pv),
        (ref.ag_h, ref.ag), (ref.wk_h, ref.wk), (ref.wv_h, ref.wv), (ref.wq_h, ref.wq), (ref.cot_h.at[0], ref.cot),
        (ref.wo_h, ref.wo), (ref.wd_h, ref.wd), (ref.fg_h, ref.fg), (ref.wg_h, ref.wg), (ref.wu_h, ref.wu),
    )
    copies = [pltpu.make_async_copy(src, dst, ref.lsem.at[i]) for i, (src, dst) in enumerate(pairs)]
    for copy in copies:
        copy.start()
    (loads.inp, loads.ids, loads.pb, loads.tp, loads.pv, loads.ag, loads.wk, loads.wv, loads.wq, loads.cot, loads.wo,
     loads.wd, loads.fg, loads.wg, loads.wu) = copies

    barrier = pltpu.get_barrier_semaphore()
    pl.semaphore_signal(barrier, 1, device_id=sibling, device_id_type=MESH)
    for o in range(1, n_mp):
        pl.semaphore_signal(barrier, 1, device_id=(mod, seq, peer_of(o)), device_id_type=MESH)

    @pl.when(seq > 0)
    def _():
        pl.semaphore_signal(barrier, 1, device_id=(mod, seq - 1, mp), device_id_type=MESH)

    @pl.when(seq < n_seq - 1)
    def _():
        pl.semaphore_signal(barrier, 1, device_id=(mod, seq + 1, mp), device_id_type=MESH)

    lower = (seq + n_seq - 1) // n_seq
    upper = (2 * n_seq - 2 - seq) // n_seq
    pl.semaphore_wait(barrier, n_mp + lower + upper)

    to_text = message(ref.inp_h.at[0], ref.inc, sibling, mod == 0)

    @pl.when(mod == 0)
    def _():
        to_text.start()

    first = ref.len_s[0, 0]
    long_first = first == LONG
    loads.ids.wait()
    loads.pb.wait()
    mirror = (
        lax.broadcasted_iota(jnp.int32, (128, 128), 0) + lax.broadcasted_iota(jnp.int32, (128, 128), 1) == 127
    ).astype(f32)
    turned_ids = nn(ref.ids[...].astype(f32).astype(bf16), mirror.astype(bf16))
    lines = turned_ids.shape[0]
    turned_ids = jnp.concatenate([turned_ids[i : i + 1, :] for i in reversed(range(lines))], axis=1)
    hot = bucket_hot(turned_ids.astype(jnp.int32))
    ref.hot[...] = hot
    rel = jnp.dot(ref.pb[...], hot, precision=lax.Precision.HIGHEST, preferred_element_type=f32)
    rel = jnp.concatenate([rel, jnp.zeros((heads, WIDE - SPANS), f32)], axis=1)
    blocks = rows // 64
    apart = ((-128, -128), (-128, -192), (-128, -192), (-64, -192))
    along = ((128, 128), (128, 128), (64, 192), (64, 192))

    def window(c):
        return pltpu.roll(rel, (WIDE - (c + 256)) % WIDE, 1)[:, :384]

    lane_row = lax.broadcasted_iota(jnp.int32, (1, rows), 1)
    patch_doc = lane_row // PDOC
    text_doc = (lane_row >= first).astype(jnp.int32)
    query_doc = jnp.where(mod == 0, patch_doc, text_doc)
    for kb in range(blocks):
        ref.win[kb] = window(-64 * kb)
        a0, a1 = (window(c - 64 * kb) for c in apart[kb])
        b0, b1 = (window(c - 64 * kb) for c in along[kb])
        ref.win[blocks + kb] = jnp.where(
            mod == 0, jnp.where(long_first, a0, a1), jnp.where(long_first, b0, b1)
        )
    for kb in range(2 * blocks):
        at = kb % blocks
        in_patch = (mod == 0) if kb < blocks else (mod == 1)
        key_doc = jnp.where(in_patch, at * 64 // PDOC, jnp.where(at * 64 >= first, 1, 0))
        same = query_doc == key_doc

        def one_bias(h, carry, kb=kb, same=same):
            line = jnp.broadcast_to(ref.win[kb, pl.ds(h, 1), :], (64, 384))
            table = pltpu.roll(line, 320, 1, stride=1, stride_axis=0)[:, :rows]
            ref.bias[h, kb * 64 : kb * 64 + 64, :] = jnp.where(same, table, -1000000000.0)
            return carry

        lax.fori_loop(0, heads, one_bias, 0)

    loads.cot.wait()

    def transposed(source, sides):
        sides.s[...] = source[:, there].T
        copy = message(sides.s, sides.r, sibling)
        copy.start()
        sides.t[...] = source[:, here].T
        return copy

    x_tan, x_na, x_nf, x_branch = (
        types.SimpleNamespace(t=ref.xt.at[i], s=ref.xs.at[i], r=ref.xr.at[i]) for i in range(4)
    )
    tan_sent = transposed(ref.cot, x_tan)

    loads.tp.wait()
    loads.pv.wait()
    loads.inp.wait()

    @pl.when(mod == 1)
    def _():
        count = patch_counts(ref.tp[...], ref.pv[...], rows).T.astype(bf16)
        to_text.wait_recv()
        ref.united[...] = nn(count, ref.inc[...])

    @pl.when(mod == 0)
    def _():
        ref.united[...] = jnp.zeros((rows, dim), f32)

    loads.ag.wait()
    attn_gain = flat(ref.ag)

    def first_norm(at):
        u = ref.united[at, :] + ref.inp[at, :].astype(f32)
        ref.united[at, :] = u
        ref.na[at, :] = (u * rms_scale(u) * attn_gain).astype(bf16)

    row_chunks(rows, 32, first_norm)
    loads.wk.wait()
    ref.kv[:, :width] = nn(ref.na[...], ref.wk[...]).astype(bf16)
    loads.wv.wait()
    ref.kv[:, width:] = nn(ref.na[...], ref.wv[...]).astype(bf16)
    kv_sent = message(ref.kv, ref.kvr, sibling)
    kv_sent.start()
    loads.wq.wait()
    ref.q[...] = nn(ref.na[...], ref.wq[...]).astype(bf16)
    ref.kvt[:, :rows] = ref.kv[...].T
    na_sent = transposed(ref.na, x_na)
    kv_sent.wait_recv()
    ref.kvt[:, rows:] = ref.kvr[...].T
    head_of = lax.broadcasted_iota(jnp.int32, (1, width), 1) // HEAD

    def head_mask(h):
        return (head_of == h).astype(f32).astype(bf16)

    def head_rows(h, base=0):
        return pl.ds(pl.multiple_of(base + h * HEAD, HEAD), HEAD)

    def head_fwd(h, carry):
        qm = ref.q[...] * head_mask(h)
        ref.qm[h] = qm
        s0 = nt(ref.kv[:, :width], qm) * 0.125 + ref.bias[h, :rows, :]
        s1 = nt(ref.kvr[:, :width], qm) * 0.125 + ref.bias[h, rows:, :]
        top = jnp.maximum(jnp.max(s0, axis=0, keepdims=True), jnp.max(s1, axis=0, keepdims=True))
        e0 = jnp.exp(s0 - top)
        e1 = jnp.exp(s1 - top)
        total = jnp.sum(e0, axis=0, keepdims=True) + jnp.sum(e1, axis=0, keepdims=True)
        scale = 1.0 / total
        p0 = e0 * scale
        p1 = e1 * scale
        ref.prob[h, :rows, :] = p0
        ref.prob[h, rows:, :] = p1
        values_t = ref.kvt[head_rows(h, width), :]
        ref.att_t[head_rows(h), :] = nn(values_t[:, :rows], p0.astype(bf16)) + nn(
            values_t[:, rows:], p1.astype(bf16)
        )
        return carry

    lax.fori_loop(0, heads, head_fwd, 0)
    ref.att[...] = ref.att_t[...].T.astype(bf16)
    att_sent = message(ref.att, ref.att_r, sibling)
    att_sent.start()
    loads.wo.wait()

    def scatter(c, product):
        ref.part[...] = product
        stage, land = ref.stage.at[c], ref.land.at[c]

        def cast(at):
            stage[at, :] = ref.part[at, :].astype(bf16)

        row_chunks(rows, 32, cast)
        copies = []
        for o in range(1, n_mp):
            to = peer_of(o)
            src = stage.at[pl.ds(pl.multiple_of(to * own_rows, own_rows), own_rows)]
            copies.append(message(src, land.at[o - 1], (mod, seq, to)))
        for copy in reversed(copies):
            copy.start()
        ref.keep[c] = ref.part[mine, :]
        return copies

    def summed(c, copies):
        for copy in copies:
            copy.wait_recv()
        total = ref.keep[c]
        for o in range(1, n_mp):
            total += ref.land[c, o - 1].astype(f32)
        return total

    def gather(c):
        whole = ref.whole.at[c]
        copies = [
            message(whole.at[mine], whole.at[mine], (mod, seq, peer_of(o))) for o in range(1, n_mp)
        ]
        for copy in reversed(copies):
            copy.start()
        return copies

    attn_sum = scatter(0, nn(ref.att[...], ref.wo[...]))
    loads.wd.wait()
    ref.hg[...] = nt(ref.cot[...], ref.wd[...])
    loads.fg.wait()
    ffn_gain = flat(ref.fg)
    middle = ref.united[mine, :] + summed(0, attn_sum)
    ref.mid[...] = middle
    ref.whole[0, mine, :] = (middle * rms_scale(middle) * ffn_gain).astype(bf16)
    nf_parts = gather(0)
    loads.wg.wait()
    loads.wu.wait()
    for copy in nf_parts:
        copy.wait_recv()
    ref.gate[...] = nt(ref.whole[0], ref.wg[...])
    ref.up[...] = nt(ref.whole[0], ref.wu[...])

    def gelu_rows(at):
        g, u, back = ref.gate[at, :], ref.up[at, :], ref.hg[at, :]
        squared = g * g
        t = jnp.tanh(ROOT * (g + 0.044715 * squared * g))
        left = 0.5 * (1.0 + t)
        gelu = left * g
        slope = left + 0.5 * g * (1.0 - t * t) * (ROOT * (1.0 + 0.134145 * squared))
        ref.hid[at, :] = (gelu * u).astype(bf16)
        ref.gg[at, :] = (back * u * slope).astype(bf16)
        ref.ug[at, :] = (back * gelu).astype(bf16)

    row_chunks(rows, 32, gelu_rows)
    ffn_in = scatter(1, nn(ref.gg[...], ref.wg[...]) + nn(ref.ug[...], ref.wu[...]))
    hid_sent = message(ref.hid, ref.hid_r, sibling)
    hid_sent.start()
    nf_sent = transposed(ref.whole.at[0], x_nf)
    gg_sent = message(ref.gg, ref.gg_r, sibling)
    ug_sent = message(ref.ug, ref.ug_r, sibling)
    gg_sent.start()
    ug_sent.start()

    after = (mod, jnp.minimum(seq + 1, n_seq - 1), mp)
    before = (mod, jnp.maximum(seq - 1, 0), mp)
    weights = []
    for g, s, a, b, o in zip(ref.wgrad, ref.wsend, ref.wleft, ref.wright, ref.wout, strict=True):
        right, left = {}, {}
        for j in range(n_seq):
            rng = pl.ds(j * block, block)
            if j > 0:
                right[j] = message(s.at[rng], a.at[rng], after, seq < j)
            if j < n_seq - 1:
                left[j] = message(s.at[rng], b.at[rng], before, seq > j)
        weights.append(types.SimpleNamespace(g=g, s=s, a=a, b=b, o=o, right=right, left=left))
    w_down, w_gate, w_up, w_proj, w_qkv = weights

    def product(w, x, pieces):
        lo = 0
        for own, other in pieces:
            size = own.shape[1]
            w.g[:, lo : lo + size] = nn(x.t[...], own[...]) + nn(x.r[...], other[...])
            lo += size

    def hop(w, step):
        @pl.when(seq == step)
        def _():
            for j in range(n_seq - 1, step, -1):
                rng = slice(j * block, (j + 1) * block)
                value = w.g[rng, :]
                if step > 0:
                    w.right[j].wait_recv()
                    value += w.a[rng, :].astype(f32)
                w.s[rng, :] = value.astype(bf16)
                w.right[j].start()

        @pl.when(seq == n_seq - 1 - step)
        def _():
            for j in range(n_seq - 1 - step):
                rng = slice(j * block, (j + 1) * block)
                value = w.g[rng, :]
                if step > 0:
                    w.left[j].wait_recv()
                    value += w.b[rng, :].astype(f32)
                w.s[rng, :] = value.astype(bf16)
                w.left[j].start()

    def arrive(w):
        for j in range(n_seq):

            @pl.when(seq == j)
            def _(j=j):
                rng = slice(j * block, (j + 1) * block)
                value = w.g[rng, :]
                if j > 0:
                    w.right[j].wait_recv()
                    value += w.a[rng, :].astype(f32)
                if j < n_seq - 1:
                    w.left[j].wait_recv()
                    value += w.b[rng, :].astype(f32)
                w.o[...] = value

    normed_grad = summed(1, ffn_in)
    middle = ref.mid[...]
    scale = rms_scale(middle)
    spread = normed_grad * ffn_gain
    ffn_gain_grad = jnp.sum(normed_grad * middle * scale, axis=0, keepdims=True)
    middle_grad = (
        ref.cot[mine, :].astype(f32)
        + scale * spread
        - middle * (scale * scale * scale) * jnp.mean(spread * middle, axis=-1, keepdims=True)
    )
    ref.mgrad[...] = middle_grad
    ref.whole[1, mine, :] = middle_grad.astype(bf16)
    branch_parts = gather(1)

    ffn_out = scatter(2, nn(ref.hid[...], ref.wd[...]))
    hid_sent.wait_recv()
    tan_sent.wait_recv()
    product(w_down, x_tan, [(ref.hid, ref.hid_r)])
    hop(w_down, 0)
    nf_sent.wait_recv()
    gg_sent.wait_recv()
    product(w_gate, x_nf, [(ref.gg, ref.gg_r)])
    hop(w_gate, 0)
    ug_sent.wait_recv()
    product(w_up, x_nf, [(ref.ug, ref.ug_r)])
    hop(w_up, 0)
    for copy in branch_parts:
        copy.wait_recv()
    ref.ga[...] = nt(ref.whole[1], ref.wo[...]).astype(bf16)
    branch_sent = transposed(ref.whole.at[1], x_branch)
    hop(w_down, 1)

    flip = (
        lax.broadcasted_iota(jnp.int32, (rows, rows), 0) // 64 == lax.broadcasted_iota(jnp.int32, (rows, rows), 1) // 64
    ) & (
        lax.broadcasted_iota(jnp.int32, (rows, rows), 0) % 64
        + lax.broadcasted_iota(jnp.int32, (rows, rows), 1) % 64
        == 63
    )
    ref.turn[...] = flip.astype(f32).astype(bf16)
    ref.dk[...] = jnp.zeros((2 * rows, width), f32)
    ref.dv[...] = jnp.zeros((2 * rows, width), f32)

    def head_bwd(h, carry):
        gm = ref.ga[...] * head_mask(h)
        p0, p1 = ref.prob[h, :rows, :], ref.prob[h, rows:, :]
        d0 = nt(ref.kv[:, width:], gm)
        d1 = nt(ref.kvr[:, width:], gm)
        inner = jnp.sum(p0 * d0, axis=0, keepdims=True) + jnp.sum(p1 * d1, axis=0, keepdims=True)
        g0 = (p0 * (d0 - inner)).astype(bf16)
        g1 = (p1 * (d1 - inner)).astype(bf16)
        keys_t = ref.kvt[head_rows(h), :]
        ref.dq_t[head_rows(h), :] = nn(keys_t[:, :rows], g0) + nn(keys_t[:, rows:], g1)
        qm = ref.qm[h]
        ref.dk[:rows, :] += nn(g0, qm)
        ref.dk[rows:, :] += nn(g1, qm)
        ref.dv[:rows, :] += nn(p0.astype(bf16), gm)
        ref.dv[rows:, :] += nn(p1.astype(bf16), gm)
        turn = ref.turn[...]
        for side, g in ((0, g0), (1, g1)):
            turned = nn(turn, g)
            for at in range(blocks):
                piece = turned[at * 64 : at * 64 + 64, :]
                piece = jnp.concatenate([piece, jnp.zeros((64, 384 - rows), f32)], axis=1)
                piece = pltpu.roll(piece, 1, 1, stride=1, stride_axis=0)
                ref.diag[side * blocks + at, pl.ds(h, 1), :] = jnp.sum(piece, axis=0, keepdims=True)
        return carry

    lax.fori_loop(0, heads, head_bwd, 0)
    ref.kvg_s[:, :width] = (ref.dk[rows:, :] * 0.125).astype(bf16)
    ref.kvg_s[:, width:] = ref.dv[rows:, :].astype(bf16)
    kvg_sent = message(ref.kvg_s, ref.kvg_r, sibling)
    kvg_sent.start()
    hop(w_gate, 1)
    att_sent.wait_recv()
    branch_sent.wait_recv()
    product(w_proj, x_branch, [(ref.att, ref.att_r)])
    hop(w_proj, 0)
    ref.dqb[...] = (ref.dq_t[...].T * 0.125).astype(bf16)
    kvg_sent.wait_recv()
    ref.dkb[...] = (ref.dk[:rows, :] * 0.125 + ref.kvg_r[:, :width].astype(f32)).astype(bf16)
    ref.dvb[...] = (ref.dv[:rows, :] + ref.kvg_r[:, width:].astype(f32)).astype(bf16)
    ref.part2[...] = (
        nt(ref.dqb[...], ref.wq[...]) + nt(ref.dkb[...], ref.wk[...]) + nt(ref.dvb[...], ref.wv[...])
    )
    attn_in = scatter(3, ref.part2[...])
    dq_sent = message(ref.dqb, ref.dq_r, sibling)
    dk_sent = message(ref.dkb, ref.dk_r, sibling)
    dv_sent = message(ref.dvb, ref.dv_r, sibling)
    for copy in (dq_sent, dk_sent, dv_sent):
        copy.start()

    def gain_rows(i, total):
        at = pl.ds(pl.multiple_of(i * 32, 32), 32)
        u = ref.united[at, :]
        return total + jnp.sum(ref.part2[at, :] * u * rms_scale(u), axis=0, keepdims=True)

    attn_gain_grad = lax.fori_loop(0, rows // 32, gain_rows, jnp.zeros((1, dim), f32))

    def unwindow(piece, c):
        grown = jnp.concatenate([piece, jnp.zeros((heads, WIDE - 384), f32)], axis=1)
        return pltpu.roll(grown, (c + 256) % WIDE, 1)

    total = jnp.zeros((heads, WIDE), f32)
    for kb in range(blocks):
        total += unwindow(ref.diag[kb], -64 * kb)
        piece = ref.diag[blocks + kb]
        a0, a1 = (unwindow(piece, c - 64 * kb) for c in apart[kb])
        b0, b1 = (unwindow(piece, c - 64 * kb) for c in along[kb])
        total += jnp.where(mod == 0, jnp.where(long_first, a0, a1), jnp.where(long_first, b0, b1))
    bias_grad = lax.dot_general(
        total[:, :SPANS], ref.hot[...], (((1,), (1,)), ((), ())), precision=lax.Precision.HIGHEST, preferred_element_type=f32
    )
    quarter = dim // 4
    for i, line in enumerate((attn_gain_grad, ffn_gain_grad)):
        for k in range(4):
            ref.small[4 * i + k : 4 * i + k + 1, :quarter] = line[:, k * quarter : (k + 1) * quarter]
    ref.small[:, quarter:] = jnp.zeros((8, 128), f32)
    ref.small[:heads, quarter : quarter + NB] = bias_grad
    small_mp = [message(ref.small, ref.small_p.at[o - 1], (mod, seq, peer_of(o))) for o in range(1, n_mp)]
    for copy in small_mp:
        copy.start()

    for copy in (na_sent, dq_sent, dk_sent, dv_sent):
        copy.wait_recv()
    product(w_qkv, x_na, [(ref.dqb, ref.dq_r), (ref.dkb, ref.dk_r), (ref.dvb, ref.dv_r)])
    hop(w_qkv, 0)
    hop(w_up, 1)
    for copy in small_mp:
        copy.wait_recv()
    gains = ref.small[:, :quarter]
    for o in range(1, n_mp):
        gains += ref.small_p[o - 1, :, :quarter]
    ref.small2[:, :quarter] = gains
    ref.small2[:, quarter:] = ref.small[:, quarter:]
    small_mod = message(ref.small2, ref.small_m, sibling)
    small_mod.start()

    normed_grad = summed(3, attn_in)
    u = ref.united[mine, :]
    scale = rms_scale(u)
    spread = normed_grad * attn_gain
    united_grad = (
        ref.mgrad[...]
        + scale * spread
        - u * (scale * scale * scale) * jnp.mean(spread * u, axis=-1, keepdims=True)
    )
    ref.whole[3, mine, :] = united_grad.astype(bf16)
    united_parts = gather(3)
    ref.whole[2, mine, :] = (ref.mid[...] + summed(2, ffn_out)).astype(bf16)
    output_parts = gather(2)
    small_mod.wait_recv()
    ref.small3[...] = ref.small2[...] + ref.small_m[...]
    small_right = message(ref.small4, ref.small_a, (mod, jnp.minimum(seq + 1, n_seq - 1), mp), seq < n_seq - 1)
    small_left = message(ref.small5, ref.small_b, (mod, jnp.maximum(seq - 1, 0), mp), seq > 0)

    def small_hop(step):
        @pl.when(seq == step)
        def _():
            value = ref.small3[...]
            if step > 0:
                small_right.wait_recv()
                value += ref.small_a[...]
            ref.small4[...] = value
            small_right.start()

        @pl.when(seq == n_seq - 1 - step)
        def _():
            value = ref.small3[...]
            if step > 0:
                small_left.wait_recv()
                value += ref.small_b[...]
            ref.small5[...] = value
            small_left.start()

    for step in range(n_seq - 1):
        small_hop(step)
    hop(w_proj, 1)
    hop(w_qkv, 1)
    for step in range(2, n_seq - 1):
        for w in weights:
            hop(w, step)

    backs = []
    for o in range(n_mp):
        who = mp if o == 0 else source_of(o)
        at = pl.ds(pl.multiple_of(who * own_rows, own_rows), own_rows)
        if o:
            united_parts[o - 1].wait_recv()
        back = message(ref.whole.at[3, at], ref.text_o.at[at], sibling, mod == 1)

        @pl.when(mod == 1)
        def _(back=back):
            back.start()

        backs.append(back)
    for copy in output_parts:
        copy.wait_recv()
    ref.out_o[...] = ref.whole[2]
    ref.own_o[...] = ref.whole[3]
    for w in weights:
        arrive(w)

    @pl.when(seq == n_seq - 1)
    def _():
        small_right.wait_recv()

    @pl.when(seq == 0)
    def _():
        small_left.wait_recv()

    ref.small_o[...] = (
        ref.small3[...]
        + jnp.where(seq > 0, ref.small_a[...], 0.0)
        + jnp.where(seq < n_seq - 1, ref.small_b[...], 0.0)
    )

    @pl.when(mod == 0)
    def _():
        for back in backs:
            back.wait_recv()

    @pl.when(mod == 1)
    def _():
        ref.text_o[...] = jnp.zeros((rows, dim), bf16)

    for cond, copy in sends:
        if cond is None:
            copy.wait_send()
        else:

            @pl.when(cond)
            def _(copy=copy):
                copy.wait_send()

    assert used[0] <= ref.ssem.shape[0]


def finish(n_seq, heads, width, ids, valid, own, text, out, gd, gg, gu, go, gqkv, small,
           o_out, o_in, o_ag, o_q, o_k, o_v, o_o, o_pb, o_fg, o_gate, o_up, o_down, hold):
    mod, seq = lax.axis_index("mod"), lax.axis_index("seq")
    rows, dim = own.shape
    place = mod * n_seq + seq
    o_out[0] = out[...]

    @pl.when(mod == 0)
    def _():
        count = patch_counts(ids[...], valid[...], rows)
        o_in[0] = own[...].astype(f32) + nn(count.astype(bf16), text[...])

    @pl.when(mod == 1)
    def _():
        o_in[0] = own[...].astype(f32)

    o_q[...] = gqkv[:, :width]
    o_k[...] = gqkv[:, width : 2 * width]
    o_v[...] = gqkv[:, 2 * width :]
    o_o[...] = go[...].T
    o_gate[...] = gg[...].T
    o_up[...] = gu[...].T
    o_down[...] = gd[...].T
    quarter = dim // 4
    part = dim // (2 * n_seq)
    for i, o_gain in enumerate((o_ag, o_fg)):
        line = jnp.concatenate([small[4 * i + k : 4 * i + k + 1, :quarter] for k in range(4)], axis=1)
        line = pltpu.roll(jnp.broadcast_to(line, (8, dim)), dim - place * part, 1)
        o_gain[...] = line[:1, :part]
    few = NB // (2 * n_seq)
    hold[...] = small[:, quarter:].T
    o_pb[...] = hold[pl.ds(place * few, few), :heads]


def per_device(n_seq, n_mp, *args):
    (inputs, text_patches, patch_valid, text_lengths, bucket_table, attn_gain, query_weight, key_weight,
     value_weight, output_weight, position_bias, ffn_gain, gate_weight, up_weight, down_weight, cotangent) = args
    rows, dim = inputs.shape[1:]
    heads = position_bias.shape[1]
    width = heads * HEAD
    ff = down_weight.shape[0]
    own_rows = rows // n_mp
    half = dim // 2
    block = half // n_seq
    text_patches, patch_valid, position_bias = text_patches.T, patch_valid.T, position_bias.T
    gate_weight, up_weight = gate_weight.T, up_weight.T
    ids = jnp.pad(bucket_table, (0, SPANS - bucket_table.shape[0])).reshape(SPANS // 128, 128)
    given = dict(
        len_s=text_lengths, inp_h=inputs, tp_h=text_patches, pv_h=patch_valid, ids_h=ids, pb_h=position_bias,
        ag_h=attn_gain.reshape(dim // 128, 128), fg_h=ffn_gain.reshape(dim // 128, 128), wq_h=query_weight, wk_h=key_weight,
        wv_h=value_weight, wo_h=output_weight, wg_h=gate_weight, wu_h=up_weight, wd_h=down_weight, cot_h=cotangent,
    )
    sizes = sizes_of(heads, ff)
    results = dict(
        wout=[((block, size), f32) for size in sizes], out_o=((rows, dim), bf16), own_o=((rows, dim), bf16),
        text_o=((rows, dim), bf16), small_o=((8, dim // 4 + 128), f32),
    )
    small = ((8, dim // 4 + 128), f32)
    sent = [((half, size), bf16) for size in sizes]
    held = dict(
        inp=((rows, dim), bf16), ids=(ids.shape, jnp.int32), hot=((NB, SPANS), f32), pb=((heads, NB), f32), tp=(text_patches.shape, jnp.int32),
        pv=(patch_valid.shape, jnp.int32), ag=((dim // 128, 128), bf16), fg=((dim // 128, 128), bf16), wq=((dim, width), bf16),
        wk=((dim, width), bf16), wv=((dim, width), bf16), wo=((width, dim), bf16), wg=((ff, dim), bf16),
        wu=((ff, dim), bf16), wd=((ff, dim), bf16), cot=((rows, dim), bf16), inc=((rows, dim), bf16),
        win=((2 * rows // 64, heads, 384), f32), diag=((2 * rows // 64, heads, 384), f32),
        bias=((heads, 2 * rows, rows), f32), prob=((heads, 2 * rows, rows), f32), xt=((4, half, rows), bf16), xs=((4, half, rows), bf16), xr=((4, half, rows), bf16),
        united=((rows, dim), f32), na=((rows, dim), bf16),
        kv=((rows, 2 * width), bf16), kvr=((rows, 2 * width), bf16), kvt=((2 * width, 2 * rows), bf16),
        q=((rows, width), bf16), qm=((heads, rows, width), bf16), att_t=((width, rows), f32), att=((rows, width), bf16),
        att_r=((rows, width), bf16), part=((rows, dim), f32), part2=((rows, dim), f32), stage=((4, rows, dim), bf16),
        land=((4, n_mp - 1, own_rows, dim), bf16), keep=((4, own_rows, dim), f32), whole=((4, rows, dim), bf16),
        hg=((rows, ff), f32), mid=((own_rows, dim), f32), mgrad=((own_rows, dim), f32), gate=((rows, ff), f32),
        up=((rows, ff), f32), ga=((rows, width), bf16), turn=((rows, rows), bf16), dk=((2 * rows, width), f32),
        dv=((2 * rows, width), f32), dq_t=((width, rows), f32), kvg_s=((rows, 2 * width), bf16),
        kvg_r=((rows, 2 * width), bf16),
    )
    held.update(
        hid=((rows, ff), bf16), hid_r=((rows, ff), bf16), gg=((rows, ff), bf16), gg_r=((rows, ff), bf16),
        ug=((rows, ff), bf16), ug_r=((rows, ff), bf16), dqb=((rows, width), bf16), dq_r=((rows, width), bf16),
        dkb=((rows, width), bf16), dk_r=((rows, width), bf16), dvb=((rows, width), bf16), dv_r=((rows, width), bf16),
        wgrad=[((half, size), f32) for size in sizes], wsend=sent, wleft=sent, wright=sent, small=small, small2=small,
        small3=small, small4=small, small5=small, small_m=small, small_a=small, small_b=small,
        small_p=((n_mp - 1,) + small[0], f32),
    )
    count = 40 + 9 * n_mp + 10 * n_seq
    order = [(name, 0) for name in given]
    out_shape, scratch = [], []
    for specs, into, make in ((results, out_shape, jax.ShapeDtypeStruct), (held, scratch, pltpu.VMEM)):
        for name, spec in specs.items():
            many = spec if isinstance(spec, list) else [spec]
            order.append((name, len(many) if isinstance(spec, list) else 0))
            into.extend(make(*one) for one in many)
    for i, size in enumerate((count, count, len(given) - 1)):
        order.append((("ssem", "rsem", "lsem")[i], 0))
        scratch.append(pltpu.SemaphoreType.DMA((size,)))
    vmem = pl.BlockSpec(memory_space=pltpu.VMEM)
    done = pl.pallas_call(
        functools.partial(mega, n_seq, n_mp, heads, order),
        out_shape=out_shape,
        in_specs=[pl.BlockSpec(memory_space=pltpu.SMEM)] + [pl.BlockSpec(memory_space=pl.ANY)] * (len(given) - 1),
        out_specs=[vmem] * len(out_shape),
        scratch_shapes=scratch,
        compiler_params=pltpu.CompilerParams(
            collective_id=0, has_side_effects=True, vmem_limit_bytes=63 * 2**20
        ),
        name="layer",
    )(*given.values())
    *wout, out, own, text, small_sum = done
    down_sum, gate_sum, up_sum, proj_sum, qkv_sum = wout
    part = dim // (2 * n_seq)
    few = NB // (2 * n_seq)
    shapes = [
        ((1, rows, dim), bf16), ((1, rows, dim), f32), ((1, part), f32), ((block, width), f32), ((block, width), f32),
        ((block, width), f32), ((width, block), f32), ((few, heads), f32), ((1, part), f32), ((ff, block), f32),
        ((ff, block), f32), ((ff, block), f32),
    ]
    outs = pl.pallas_call(
        functools.partial(finish, n_seq, heads, width),
        out_shape=[jax.ShapeDtypeStruct(*spec) for spec in shapes],
        in_specs=[vmem] * 11,
        out_specs=[vmem] * 12,
        scratch_shapes=[pltpu.VMEM((128, 8), f32)],
        compiler_params=pltpu.CompilerParams(vmem_limit_bytes=63 * 2**20),
        name="finish",
    )(
        text_patches, patch_valid, own, text, out, down_sum, gate_sum, up_sum, proj_sum, qkv_sum, small_sum
    )
    outs = list(outs)
    for i in (9, 10):
        outs[i] = outs[i].T
    outs[2] = outs[2].reshape(part)
    outs[8] = outs[8].reshape(part)
    return tuple(outs)


def solution(mesh):
    group = ("mod", "seq")
    in_specs = (
        P("mod", "seq", None), P("seq", None), P("seq", None), P("seq", None), P(), P(), P(None, "mp"), P(None, "mp"),
        P(None, "mp"), P("mp", None), P(None, "mp"), P(), P(None, "mp"), P(None, "mp"), P("mp", None),
        P("mod", "seq", None),
    )
    out_specs = (
        P("mod", "seq", None), P("mod", "seq", None), P(group), P(group, "mp"), P(group, "mp"), P(group, "mp"),
        P("mp", group), P(group, "mp"), P(group), P(group, "mp"), P(group, "mp"), P("mp", group),
    )
    body = functools.partial(per_device, mesh.shape["seq"], mesh.shape["mp"])
    return jax.shard_map(body, mesh=mesh, in_specs=in_specs, out_specs=out_specs, check_vma=False)
```

time: 838 us -> 129 us (0.15)
  waiting for transfers between devices: 323 us -> 0 us
  matrix products: 318 us -> 0 us
  Pallas kernels: 0 us -> 127 us
  local copies, waits for them, and re-layouts: 105 us -> 1.28 us
  other arithmetic: 33.7 us -> 0 us
  blocking collectives: 31.7 us -> 0 us
  between operations: 16.1 us -> 0.81 us
    dot_general x83 -> x0, matrix products: 318 us -> none  [the longest x10 142 us: toeplitz_block(): jnp.einsum('abs,sh->hab', diagonal_hot(start), rel_bias, precision=highest)]
    reduce_scatter x7 -> x0, waiting for transfers between devices: 218 us -> none  [the longest x1 66 us: per_device(): lax.psum_scatter(up_weight_grad, ('mod', 'seq'), scatter_dimension=0, til...]
    pallas_call x0 -> x2, Pallas kernels: none -> 127 us  [the longest x1 123 us: per_device(): pl.pallas_call(functools.partial(mega, n_seq, n_mp, heads, order), out_sh...]
    psum x3 -> x0, waiting for transfers between devices: 104 us -> none  [the longest x1 54 us: per_device(): middle = united_rows + lax.psum(attn_terms, 'mp')]
    dynamic_update_slice x16 -> x0, local copies, waits for them, and re-layouts: 57.6 us -> none  [the longest x8 47.2 us: per_device(): lax.map(backward_head, (head_queries, head_keys, head_values, bias_map, s...]
    unnamed x1 -> x0, blocking collectives: 31.7 us -> none
    dynamic_slice x24 -> x0, local copies, waits for them, and re-layouts: 28.4 us -> none  [the longest x20 25.5 us: per_device(): lax.map(toeplitz_block, block_starts)]
    add x21 -> x0, other arithmetic: 13.3 us -> none  [the longest x20 13 us: diagonal_hot(): first_pos = start + jnp.arange(pos_block, dtype=jnp.int32)]
  transfers between devices with their start and end apart: 16 -> 0, of which waited for: 7 -> 0; matrix products, arithmetic and copies ran while one was open for 39% -> 0% of each run, Pallas kernels for 0% -> 0%
where the time goes in v1:
time: 129 us
  Pallas kernels  127 us (98%)
    pallas_call x1, Pallas kernels, per_device(): pl.pallas_call(functools.partial(mega, n_seq, n_mp, heads, order), out_sh...  123 us
    pallas_call x1, Pallas kernels, per_device(): pl.pallas_call(functools.partial(finish, n_seq, heads, width), out_shape=...  3.97 us

profile of v1, /device:TPU:0, one launch (start us, length us, event | category | flops | bytes accessed | tf_op | source)
XLA Modules:
  0.0 128.9 jit_solution(3995197799650053320)
XLA Ops:
  0.6 1.3 pad_bitcast_fusion.refs_4_
  1.9 122.8 %layer.1 = (f32[128,704]{1,0:T(8,128)}, f32[128,704]{1,0:T(8,128)}, f32[128,704]{1,0:T(8,128)}, f32[128,256]{1,0:T(8,128)}, f32[128,768]{1,0:T(8,128)}, /*index=...) custom-call(s32[1,2]{1,0:T(1,128)} %refs_0_.1, ...), custom_call_target="tpu_custom_call" | custom-call | tf_op jit(solution)/shard_map/layer/pallas_call | solution.py:737
  124.8 4.0 %finish.1 = (bf16[1,256,1024]{2,1,0:T(8,128)(2,1)}, f32[1,256,1024]{2,1,0:T(8,128)}, f32[1,128]{1,0:T(1,128)}, f32[128,256]{1,0:T(8,128)}, f32[128,256]{1,0:T(8,...) custom-call(s32[4,256]{1,0:T(4,128)} %bitcast.16, ...), custom_call_target="tpu_custom_call" | custom-call | tf_op jit(solution)/shard_map/finish/pallas_call | solution.py:757

commit v2 on v1

--- a/solution.py
+++ b/solution.py
@@ -80,6 +80,16 @@
     sibling = (1 - mod, seq, mp)
     used = [0]
     sends = []
+    is_end = (seq == 0) | (seq == n_seq - 1)
+    not_end = (seq > 0) & (seq < n_seq - 1)
+    is_inner = (seq == 1) | (seq == n_seq - 2)
+    inner = (mod, seq + 1 - 2 * (seq // (n_seq - 1)), mp)
+
+    def when(cond, body):
+        if cond is None:
+            body()
+        else:
+            pl.when(cond)(body)
 
     def peer_of(o):
         if n_mp == 4:
@@ -122,23 +132,18 @@
     for o in range(1, n_mp):
         pl.semaphore_signal(barrier, 1, device_id=(mod, seq, peer_of(o)), device_id_type=MESH)
 
-    @pl.when(seq > 0)
-    def _():
-        pl.semaphore_signal(barrier, 1, device_id=(mod, seq - 1, mp), device_id_type=MESH)
-
-    @pl.when(seq < n_seq - 1)
-    def _():
-        pl.semaphore_signal(barrier, 1, device_id=(mod, seq + 1, mp), device_id_type=MESH)
-
-    lower = (seq + n_seq - 1) // n_seq
-    upper = (2 * n_seq - 2 - seq) // n_seq
-    pl.semaphore_wait(barrier, n_mp + lower + upper)
+    for o in range(1, n_seq):
+        pl.semaphore_signal(barrier, 1, device_id=(mod, (seq + o) % n_seq, mp), device_id_type=MESH)
+    pl.semaphore_wait(barrier, n_mp + n_seq - 1)
 
     to_text = message(ref.inp_h.at[0], ref.inc, sibling, mod == 0)
 
     @pl.when(mod == 0)
     def _():
         to_text.start()
+
+    cot_end = message(ref.cot_h.at[0], ref.cot_e, inner, is_end)
+    when(is_end, cot_end.start)
 
     first = ref.len_s[0, 0]
     long_first = first == LONG
@@ -188,17 +193,21 @@
 
     loads.cot.wait()
 
-    def transposed(source, sides):
-        sides.s[...] = source[:, there].T
-        copy = message(sides.s, sides.r, sibling)
-        copy.start()
-        sides.t[...] = source[:, here].T
+    def transposed(source, sides, cond=None):
+        copy = message(sides.s, sides.r, sibling, cond)
+
+        def body():
+            sides.s[...] = source[:, there].T
+            copy.start()
+            sides.t[...] = source[:, here].T
+
+        when(cond, body)
         return copy
 
-    x_tan, x_na, x_nf, x_branch = (
-        types.SimpleNamespace(t=ref.xt.at[i], s=ref.xs.at[i], r=ref.xr.at[i]) for i in range(4)
-    )
-    tan_sent = transposed(ref.cot, x_tan)
+    x_tan, x_na, x_nf, x_branch, x_tan_e, x_nf_e = (
+        types.SimpleNamespace(t=ref.xt.at[i], s=ref.xs.at[i], r=ref.xr.at[i]) for i in range(6)
+    )
+    tan_sent = transposed(ref.cot, x_tan, not_end)
 
     loads.tp.wait()
     loads.pv.wait()
@@ -269,22 +278,17 @@
     att_sent.start()
     loads.wo.wait()
 
-    def scatter(c, product):
-        ref.part[...] = product
+    def scatter(c, rows_of, hold=False):
         stage, land = ref.stage.at[c], ref.land.at[c]
-
-        def cast(at):
-            stage[at, :] = ref.part[at, :].astype(bf16)
-
-        row_chunks(rows, 32, cast)
         copies = []
-        for o in range(1, n_mp):
+        for o in range(n_mp - 1, 0, -1):
             to = peer_of(o)
-            src = stage.at[pl.ds(pl.multiple_of(to * own_rows, own_rows), own_rows)]
-            copies.append(message(src, land.at[o - 1], (mod, seq, to)))
-        for copy in reversed(copies):
-            copy.start()
-        ref.keep[c] = ref.part[mine, :]
+            at = pl.ds(pl.multiple_of(to * own_rows, own_rows), own_rows)
+            stage[at, :] = rows_of(at).astype(bf16)
+            copies.append(message(stage.at[at], land.at[o - 1], (mod, seq, to)))
+            if not hold:
+                copies[-1].start()
+        ref.keep[c] = rows_of(mine)
         return copies
 
     def summed(c, copies):
@@ -304,7 +308,7 @@
             copy.start()
         return copies
 
-    attn_sum = scatter(0, nn(ref.att[...], ref.wo[...]))
+    attn_sum = scatter(0, lambda at: nn(ref.att[at, :], ref.wo[...]))
     loads.wd.wait()
     ref.hg[...] = nt(ref.cot[...], ref.wd[...])
     loads.fg.wait()
@@ -313,59 +317,85 @@
     ref.mid[...] = middle
     ref.whole[0, mine, :] = (middle * rms_scale(middle) * ffn_gain).astype(bf16)
     nf_parts = gather(0)
+
+    def to_inner(who):
+        at = pl.ds(pl.multiple_of(who * own_rows, own_rows), own_rows)
+        copy = message(ref.whole.at[0, at], ref.nf_e.at[at], inner, is_end)
+        when(is_end, copy.start)
+        return copy
+
+    nf_end = [to_inner(mp)]
+    tan_e_sent = message(x_tan_e.s, x_tan_e.r, sibling, is_inner)
+
+    @pl.when(is_inner)
+    def _():
+        cot_end.wait_recv()
+        x_tan_e.s[...] = ref.cot_e[:, there].T
+        tan_e_sent.start()
+        x_tan_e.t[...] = ref.cot_e[:, here].T
+        ref.hg_e[...] = nt(ref.cot_e[...], ref.wd[...])
+
     loads.wg.wait()
     loads.wu.wait()
-    for copy in nf_parts:
+    for o, copy in enumerate(nf_parts, 1):
         copy.wait_recv()
+        nf_end.append(to_inner(source_of(o)))
     ref.gate[...] = nt(ref.whole[0], ref.wg[...])
     ref.up[...] = nt(ref.whole[0], ref.wu[...])
 
-    def gelu_rows(at):
-        g, u, back = ref.gate[at, :], ref.up[at, :], ref.hg[at, :]
+    def gelu_rows(at, back_ref=ref.hg, hid=ref.hid, gg=ref.gg, ug=ref.ug):
+        g, u, back = ref.gate[at, :], ref.up[at, :], back_ref[at, :]
         squared = g * g
         t = jnp.tanh(ROOT * (g + 0.044715 * squared * g))
         left = 0.5 * (1.0 + t)
         gelu = left * g
         slope = left + 0.5 * g * (1.0 - t * t) * (ROOT * (1.0 + 0.134145 * squared))
-        ref.hid[at, :] = (gelu * u).astype(bf16)
-        ref.gg[at, :] = (back * u * slope).astype(bf16)
-        ref.ug[at, :] = (back * gelu).astype(bf16)
+        hid[at, :] = (gelu * u).astype(bf16)
+        gg[at, :] = (back * u * slope).astype(bf16)
+        ug[at, :] = (back * gelu).astype(bf16)
 
     row_chunks(rows, 32, gelu_rows)
-    ffn_in = scatter(1, nn(ref.gg[...], ref.wg[...]) + nn(ref.ug[...], ref.wu[...]))
-    hid_sent = message(ref.hid, ref.hid_r, sibling)
-    hid_sent.start()
-    nf_sent = transposed(ref.whole.at[0], x_nf)
-    gg_sent = message(ref.gg, ref.gg_r, sibling)
-    ug_sent = message(ref.ug, ref.ug_r, sibling)
-    gg_sent.start()
-    ug_sent.start()
+    ffn_in = scatter(1, lambda at: nn(ref.gg[at, :], ref.wg[...]) + nn(ref.ug[at, :], ref.wu[...]))
+    hid_sent = message(ref.hid, ref.hid_r, sibling, not_end)
+    gg_sent = message(ref.gg, ref.gg_r, sibling, not_end)
+    ug_sent = message(ref.ug, ref.ug_r, sibling, not_end)
+    when(not_end, hid_sent.start)
+    nf_sent = transposed(ref.whole.at[0], x_nf, not_end)
+    when(not_end, gg_sent.start)
+    when(not_end, ug_sent.start)
 
     after = (mod, jnp.minimum(seq + 1, n_seq - 1), mp)
     before = (mod, jnp.maximum(seq - 1, 0), mp)
     weights = []
-    for g, s, a, b, o in zip(ref.wgrad, ref.wsend, ref.wleft, ref.wright, ref.wout, strict=True):
+    ends = (1, 1, 1, 0, 0)
+    for e, g, s, a, b, o in zip(ends, ref.wgrad, ref.wsend, ref.wleft, ref.wright, ref.wout, strict=True):
         right, left = {}, {}
         for j in range(n_seq):
             rng = pl.ds(j * block, block)
-            if j > 0:
-                right[j] = message(s.at[rng], a.at[rng], after, seq < j)
-            if j < n_seq - 1:
-                left[j] = message(s.at[rng], b.at[rng], before, seq > j)
-        weights.append(types.SimpleNamespace(g=g, s=s, a=a, b=b, o=o, right=right, left=left))
+            if j > e:
+                right[j] = message(s.at[rng], a.at[rng], after, (seq >= e) & (seq < j))
+            if j < n_seq - 1 - e:
+                left[j] = message(s.at[rng], b.at[rng], before, (seq < n_seq - e) & (seq > j))
+        weights.append(types.SimpleNamespace(e=e, g=g, s=s, a=a, b=b, o=o, right=right, left=left))
     w_down, w_gate, w_up, w_proj, w_qkv = weights
 
-    def product(w, x, pieces):
+    def product(w, x, pieces, more=False):
         lo = 0
         for own, other in pieces:
             size = own.shape[1]
-            w.g[:, lo : lo + size] = nn(x.t[...], own[...]) + nn(x.r[...], other[...])
+            both = nn(x.t[...], own[...]) + nn(x.r[...], other[...])
+            if more:
+                both += w.g[:, lo : lo + size]
+            w.g[:, lo : lo + size] = both
             lo += size
 
     def hop(w, step):
-        @pl.when(seq == step)
+        if step >= n_seq - 1 - w.e:
+            return
+
+        @pl.when(seq == w.e + step)
         def _():
-            for j in range(n_seq - 1, step, -1):
+            for j in range(n_seq - 1, w.e + step, -1):
                 rng = slice(j * block, (j + 1) * block)
                 value = w.g[rng, :]
                 if step > 0:
@@ -374,9 +404,9 @@
                 w.s[rng, :] = value.astype(bf16)
                 w.right[j].start()
 
-        @pl.when(seq == n_seq - 1 - step)
+        @pl.when(seq == n_seq - 1 - w.e - step)
         def _():
-            for j in range(n_seq - 1 - step):
+            for j in range(n_seq - 1 - w.e - step):
                 rng = slice(j * block, (j + 1) * block)
                 value = w.g[rng, :]
                 if step > 0:
@@ -391,14 +421,53 @@
             @pl.when(seq == j)
             def _(j=j):
                 rng = slice(j * block, (j + 1) * block)
-                value = w.g[rng, :]
-                if j > 0:
+                value = w.g[rng, :] if w.e <= j < n_seq - w.e else jnp.zeros(w.o.shape, f32)
+                if j > w.e:
                     w.right[j].wait_recv()
                     value += w.a[rng, :].astype(f32)
-                if j < n_seq - 1:
+                if j < n_seq - 1 - w.e:
                     w.left[j].wait_recv()
                     value += w.b[rng, :].astype(f32)
                 w.o[...] = value
+
+    hid_e_sent = message(ref.hid_e, ref.hid_er, sibling, is_inner)
+    gg_e_sent = message(ref.gg_e, ref.gg_er, sibling, is_inner)
+    ug_e_sent = message(ref.ug_e, ref.ug_er, sibling, is_inner)
+    nf_e_sent = message(x_nf_e.s, x_nf_e.r, sibling, is_inner)
+
+    @pl.when(is_inner)
+    def _():
+        for copy in nf_end:
+            copy.wait_recv()
+        ref.gate[...] = nt(ref.nf_e[...], ref.wg[...])
+        ref.up[...] = nt(ref.nf_e[...], ref.wu[...])
+        row_chunks(rows, 32, lambda at: gelu_rows(at, ref.hg_e, ref.hid_e, ref.gg_e, ref.ug_e))
+        hid_e_sent.start()
+        x_nf_e.s[...] = ref.nf_e[:, there].T
+        nf_e_sent.start()
+        gg_e_sent.start()
+        ug_e_sent.start()
+        x_nf_e.t[...] = ref.nf_e[:, here].T
+
+    @pl.when(not_end)
+    def _():
+        hid_sent.wait_recv()
+        tan_sent.wait_recv()
+        product(w_down, x_tan, [(ref.hid, ref.hid_r)])
+        nf_sent.wait_recv()
+        gg_sent.wait_recv()
+        product(w_gate, x_nf, [(ref.gg, ref.gg_r)])
+        ug_sent.wait_recv()
+        product(w_up, x_nf, [(ref.ug, ref.ug_r)])
+
+    def end_products(w, x, pieces, needs):
+        @pl.when(is_inner)
+        def _():
+            for copy in needs:
+                copy.wait_recv()
+            product(w, x, pieces, more=True)
+
+        hop(w, 0)
 
     normed_grad = summed(1, ffn_in)
     middle = ref.mid[...]
@@ -414,23 +483,16 @@
     ref.whole[1, mine, :] = middle_grad.astype(bf16)
     branch_parts = gather(1)
 
-    ffn_out = scatter(2, nn(ref.hid[...], ref.wd[...]))
-    hid_sent.wait_recv()
-    tan_sent.wait_recv()
-    product(w_down, x_tan, [(ref.hid, ref.hid_r)])
-    hop(w_down, 0)
-    nf_sent.wait_recv()
-    gg_sent.wait_recv()
-    product(w_gate, x_nf, [(ref.gg, ref.gg_r)])
-    hop(w_gate, 0)
-    ug_sent.wait_recv()
-    product(w_up, x_nf, [(ref.ug, ref.ug_r)])
-    hop(w_up, 0)
+    end_products(w_down, x_tan_e, [(ref.hid_e, ref.hid_er)], (hid_e_sent, tan_e_sent))
+    end_products(w_gate, x_nf_e, [(ref.gg_e, ref.gg_er)], (gg_e_sent, nf_e_sent))
+    end_products(w_up, x_nf_e, [(ref.ug_e, ref.ug_er)], (ug_e_sent,))
+    ffn_out = scatter(2, lambda at: nn(ref.hid[at, :], ref.wd[...]), hold=True)
     for copy in branch_parts:
         copy.wait_recv()
+    for copy in ffn_out:
+        copy.start()
     ref.ga[...] = nt(ref.whole[1], ref.wo[...]).astype(bf16)
     branch_sent = transposed(ref.whole.at[1], x_branch)
-    hop(w_down, 1)
 
     flip = (
         lax.broadcasted_iota(jnp.int32, (rows, rows), 0) // 64 == lax.broadcasted_iota(jnp.int32, (rows, rows), 1) // 64
@@ -473,7 +535,8 @@
     ref.kvg_s[:, width:] = ref.dv[rows:, :].astype(bf16)
     kvg_sent = message(ref.kvg_s, ref.kvg_r, sibling)
     kvg_sent.start()
-    hop(w_gate, 1)
+    ref.whole[2, mine, :] = (ref.mid[...] + summed(2, ffn_out)).astype(bf16)
+    output_parts = gather(2)
     att_sent.wait_recv()
     branch_sent.wait_recv()
     product(w_proj, x_branch, [(ref.att, ref.att_r)])
@@ -482,10 +545,13 @@
     kvg_sent.wait_recv()
     ref.dkb[...] = (ref.dk[:rows, :] * 0.125 + ref.kvg_r[:, :width].astype(f32)).astype(bf16)
     ref.dvb[...] = (ref.dv[:rows, :] + ref.kvg_r[:, width:].astype(f32)).astype(bf16)
-    ref.part2[...] = (
-        nt(ref.dqb[...], ref.wq[...]) + nt(ref.dkb[...], ref.wk[...]) + nt(ref.dvb[...], ref.wv[...])
-    )
-    attn_in = scatter(3, ref.part2[...])
+
+    def attn_rows(at):
+        rows_in = nt(ref.dqb[at, :], ref.wq[...]) + nt(ref.dkb[at, :], ref.wk[...]) + nt(ref.dvb[at, :], ref.wv[...])
+        ref.part2[at, :] = rows_in
+        return rows_in
+
+    attn_in = scatter(3, attn_rows)
     dq_sent = message(ref.dqb, ref.dq_r, sibling)
     dk_sent = message(ref.dkb, ref.dk_r, sibling)
     dv_sent = message(ref.dvb, ref.dv_r, sibling)
@@ -527,7 +593,9 @@
         copy.wait_recv()
     product(w_qkv, x_na, [(ref.dqb, ref.dq_r), (ref.dkb, ref.dk_r), (ref.dvb, ref.dv_r)])
     hop(w_qkv, 0)
-    hop(w_up, 1)
+    hop(w_down, 1)
+    hop(w_proj, 1)
+    hop(w_gate, 1)
     for copy in small_mp:
         copy.wait_recv()
     gains = ref.small[:, :quarter]
@@ -549,35 +617,14 @@
     )
     ref.whole[3, mine, :] = united_grad.astype(bf16)
     united_parts = gather(3)
-    ref.whole[2, mine, :] = (ref.mid[...] + summed(2, ffn_out)).astype(bf16)
-    output_parts = gather(2)
     small_mod.wait_recv()
     ref.small3[...] = ref.small2[...] + ref.small_m[...]
-    small_right = message(ref.small4, ref.small_a, (mod, jnp.minimum(seq + 1, n_seq - 1), mp), seq < n_seq - 1)
-    small_left = message(ref.small5, ref.small_b, (mod, jnp.maximum(seq - 1, 0), mp), seq > 0)
-
-    def small_hop(step):
-        @pl.when(seq == step)
-        def _():
-            value = ref.small3[...]
-            if step > 0:
-                small_right.wait_recv()
-                value += ref.small_a[...]
-            ref.small4[...] = value
-            small_right.start()
-
-        @pl.when(seq == n_seq - 1 - step)
-        def _():
-            value = ref.small3[...]
-            if step > 0:
-                small_left.wait_recv()
-                value += ref.small_b[...]
-            ref.small5[...] = value
-            small_left.start()
-
-    for step in range(n_seq - 1):
-        small_hop(step)
-    hop(w_proj, 1)
+    small_seq = [
+        message(ref.small3, ref.small_q.at[o - 1], (mod, (seq + o) % n_seq, mp)) for o in range(1, n_seq)
+    ]
+    for copy in small_seq:
+        copy.start()
+    hop(w_up, 1)
     hop(w_qkv, 1)
     for step in range(2, n_seq - 1):
         for w in weights:
@@ -603,19 +650,11 @@
     for w in weights:
         arrive(w)
 
-    @pl.when(seq == n_seq - 1)
-    def _():
-        small_right.wait_recv()
-
-    @pl.when(seq == 0)
-    def _():
-        small_left.wait_recv()
-
-    ref.small_o[...] = (
-        ref.small3[...]
-        + jnp.where(seq > 0, ref.small_a[...], 0.0)
-        + jnp.where(seq < n_seq - 1, ref.small_b[...], 0.0)
-    )
+    total = ref.small3[...]
+    for i, copy in enumerate(small_seq):
+        copy.wait_recv()
+        total += ref.small_q[i]
+    ref.small_o[...] = total
 
     @pl.when(mod == 0)
     def _():
@@ -703,13 +742,15 @@
         wk=((dim, width), bf16), wv=((dim, width), bf16), wo=((width, dim), bf16), wg=((ff, dim), bf16),
         wu=((ff, dim), bf16), wd=((ff, dim), bf16), cot=((rows, dim), bf16), inc=((rows, dim), bf16),
         win=((2 * rows // 64, heads, 384), f32), diag=((2 * rows // 64, heads, 384), f32),
-        bias=((heads, 2 * rows, rows), f32), prob=((heads, 2 * rows, rows), f32), xt=((4, half, rows), bf16), xs=((4, half, rows), bf16), xr=((4, half, rows), bf16),
+        bias=((heads, 2 * rows, rows), f32), prob=((heads, 2 * rows, rows), f32), xt=((6, half, rows), bf16), xs=((6, half, rows), bf16), xr=((6, half, rows), bf16),
         united=((rows, dim), f32), na=((rows, dim), bf16),
         kv=((rows, 2 * width), bf16), kvr=((rows, 2 * width), bf16), kvt=((2 * width, 2 * rows), bf16),
         q=((rows, width), bf16), qm=((heads, rows, width), bf16), att_t=((width, rows), f32), att=((rows, width), bf16),
-        att_r=((rows, width), bf16), part=((rows, dim), f32), part2=((rows, dim), f32), stage=((4, rows, dim), bf16),
+        att_r=((rows, width), bf16), part2=((rows, dim), f32), stage=((4, rows, dim), bf16),
         land=((4, n_mp - 1, own_rows, dim), bf16), keep=((4, own_rows, dim), f32), whole=((4, rows, dim), bf16),
-        hg=((rows, ff), f32), mid=((own_rows, dim), f32), mgrad=((own_rows, dim), f32), gate=((rows, ff), f32),
+        cot_e=((rows, dim), bf16), nf_e=((rows, dim), bf16), hg_e=((rows, ff), f32), hid_e=((rows, ff), bf16),
+        hid_er=((rows, ff), bf16), gg_e=((rows, ff), bf16), gg_er=((rows, ff), bf16), ug_e=((rows, ff), bf16),
+        ug_er=((rows, ff), bf16), hg=((rows, ff), f32), mid=((own_rows, dim), f32), mgrad=((own_rows, dim), f32), gate=((rows, ff), f32),
         up=((rows, ff), f32), ga=((rows, width), bf16), turn=((rows, rows), bf16), dk=((2 * rows, width), f32),
         dv=((2 * rows, width), f32), dq_t=((width, rows), f32), kvg_s=((rows, 2 * width), bf16),
         kvg_r=((rows, 2 * width), bf16),
@@ -719,7 +760,7 @@
         ug=((rows, ff), bf16), ug_r=((rows, ff), bf16), dqb=((rows, width), bf16), dq_r=((rows, width), bf16),
         dkb=((rows, width), bf16), dk_r=((rows, width), bf16), dvb=((rows, width), bf16), dv_r=((rows, width), bf16),
         wgrad=[((half, size), f32) for size in sizes], wsend=sent, wleft=sent, wright=sent, small=small, small2=small,
-        small3=small, small4=small, small5=small, small_m=small, small_a=small, small_b=small,
+        small3=small, small_m=small, small_q=((n_seq - 1,) + small[0], f32),
         small_p=((n_mp - 1,) + small[0], f32),
     )
     count = 40 + 9 * n_mp + 10 * n_seq

time: 129 us -> 97.1 us (0.75)
  Pallas kernels: 127 us -> 94.8 us
    pallas_call x1, Pallas kernels: 123 us -> 90.9 us  [per_device(): pl.pallas_call(functools.partial(mega, n_seq, n_mp, heads, order), out_sh...]
where the time goes in v2:
time: 97.1 us; the launch traced here: 96.9 us
  Pallas kernels  94.8 us (98%)
  local copies, waits for them, and re-layouts  1.28 us (1%)
    pallas_call x1, Pallas kernels, per_device(): pl.pallas_call(functools.partial(mega, n_seq, n_mp, heads, order), out_sh...  90.9 us
    pallas_call x1, Pallas kernels, per_device(): pl.pallas_call(functools.partial(finish, n_seq, heads, width), out_shape=...  3.97 us

profile of v2, /device:TPU:0, one launch (start us, length us, event | category | flops | bytes accessed | tf_op | source)
XLA Modules:
  0.0 96.9 jit_solution(13986409318881381844)
XLA Ops:
  0.6 1.3 %pad_bitcast_fusion.refs_4_ = s32[5,128]{1,0:T(8,128)} fusion(s32[639]{0:T(1024)} %param.20), kind=kLoop, calls=%fused_computation | loop fusion | bytes 5116 | tf_op jit(solution)/shard_map/reshape | solution.py:726
  1.9 90.9 %layer.1 = (f32[128,704]{1,0:T(8,128)}, f32[128,704]{1,0:T(8,128)}, f32[128,704]{1,0:T(8,128)}, f32[128,256]{1,0:T(8,128)}, f32[128,768]{1,0:T(8,128)}, /*index=...) custom-call(s32[1,2]{1,0:T(1,128)} %refs_0_.1, ...), custom_call_target="tpu_custom_call" | custom-call | tf_op jit(solution)/shard_map/layer/pallas_call | solution.py:778
  92.8 4.0 %finish.1 = (bf16[1,256,1024]{2,1,0:T(8,128)(2,1)}, f32[1,256,1024]{2,1,0:T(8,128)}, f32[1,128]{1,0:T(1,128)}, f32[128,256]{1,0:T(8,128)}, f32[128,256]{1,0:T(8,...) custom-call(s32[4,256]{1,0:T(4,128)} %bitcast.16, ...), custom_call_target="tpu_custom_call" | custom-call | tf_op jit(solution)/shard_map/finish/pallas_call | solution.py:798

commit v3 on v2

--- a/solution.py
+++ b/solution.py
@@ -10,6 +10,7 @@
 
 MESH = pl.DeviceIdType.MESH
 EPS = 1e-06
+PARTS = 2
 ROOT = 0.7978845608028654
 HEAD = 64
 NB = 32
@@ -33,9 +34,9 @@
     return lax.rsqrt(jnp.mean(x * x, axis=-1, keepdims=True) + EPS)
 
 
-def row_chunks(total, step, body):
+def row_chunks(first, total, step, body):
     def one(i, carry):
-        body(pl.ds(pl.multiple_of(i * step, step), step))
+        body(pl.ds(pl.multiple_of(first + i * step, step), step))
         return carry
 
     lax.fori_loop(0, total // step, one, 0)
@@ -60,7 +61,7 @@
 
 def sizes_of(heads, ff):
     width = heads * HEAD
-    return (ff, ff, ff, width, 3 * width)
+    return (ff, ff, ff, width, width, width, width)
 
 
 def mega(n_seq, n_mp, heads, order, *refs):
@@ -73,8 +74,19 @@
     ff = ref.wg.shape[0]
     half = dim // 2
     block = half // n_seq
-    own_rows = rows // n_mp
-    mine = pl.ds(pl.multiple_of(mp * own_rows, own_rows), own_rows)
+    part_rows = rows // PARTS
+    own_rows = part_rows // n_mp
+    parts = range(PARTS)
+
+    def part(k):
+        return slice(k * part_rows, (k + 1) * part_rows)
+
+    def share(k, who):
+        return pl.ds(pl.multiple_of(k * part_rows + who * own_rows, own_rows), own_rows)
+
+    def kept(k):
+        return slice(k * own_rows, (k + 1) * own_rows)
+
     here = pl.ds(pl.multiple_of(mod * half, half), half)
     there = pl.ds(pl.multiple_of((1 - mod) * half, half), half)
     sibling = (1 - mod, seq, mp)
@@ -186,7 +198,7 @@
         def one_bias(h, carry, kb=kb, same=same):
             line = jnp.broadcast_to(ref.win[kb, pl.ds(h, 1), :], (64, 384))
             table = pltpu.roll(line, 320, 1, stride=1, stride_axis=0)[:, :rows]
-            ref.bias[h, kb * 64 : kb * 64 + 64, :] = jnp.where(same, table, -1000000000.0)
+            ref.prob[h, kb * 64 : kb * 64 + 64, :] = jnp.where(same, table, -1000000000.0)
             return carry
 
         lax.fori_loop(0, heads, one_bias, 0)
@@ -231,7 +243,7 @@
         ref.united[at, :] = u
         ref.na[at, :] = (u * rms_scale(u) * attn_gain).astype(bf16)
 
-    row_chunks(rows, 32, first_norm)
+    row_chunks(0, rows, 32, first_norm)
     loads.wk.wait()
     ref.kv[:, :width] = nn(ref.na[...], ref.wk[...]).astype(bf16)
     loads.wv.wait()
@@ -252,11 +264,12 @@
     def head_rows(h, base=0):
         return pl.ds(pl.multiple_of(base + h * HEAD, HEAD), HEAD)
 
-    def head_fwd(h, carry):
-        qm = ref.q[...] * head_mask(h)
-        ref.qm[h] = qm
-        s0 = nt(ref.kv[:, :width], qm) * 0.125 + ref.bias[h, :rows, :]
-        s1 = nt(ref.kvr[:, :width], qm) * 0.125 + ref.bias[h, rows:, :]
+    def head_fwd(k, h, carry):
+        at = part(k)
+        qm = ref.q[at, :] * head_mask(h)
+        ref.qm[h, at, :] = qm
+        s0 = nt(ref.kv[:, :width], qm) * 0.125 + ref.prob[h, :rows, at]
+        s1 = nt(ref.kvr[:, :width], qm) * 0.125 + ref.prob[h, rows:, at]
         top = jnp.maximum(jnp.max(s0, axis=0, keepdims=True), jnp.max(s1, axis=0, keepdims=True))
         e0 = jnp.exp(s0 - top)
         e1 = jnp.exp(s1 - top)
@@ -264,67 +277,68 @@
         scale = 1.0 / total
         p0 = e0 * scale
         p1 = e1 * scale
-        ref.prob[h, :rows, :] = p0
-        ref.prob[h, rows:, :] = p1
+        ref.prob[h, :rows, at] = p0
+        ref.prob[h, rows:, at] = p1
         values_t = ref.kvt[head_rows(h, width), :]
-        ref.att_t[head_rows(h), :] = nn(values_t[:, :rows], p0.astype(bf16)) + nn(
+        ref.att_t[head_rows(h), at] = nn(values_t[:, :rows], p0.astype(bf16)) + nn(
             values_t[:, rows:], p1.astype(bf16)
         )
         return carry
 
-    lax.fori_loop(0, heads, head_fwd, 0)
-    ref.att[...] = ref.att_t[...].T.astype(bf16)
-    att_sent = message(ref.att, ref.att_r, sibling)
-    att_sent.start()
-    loads.wo.wait()
-
-    def scatter(c, rows_of, hold=False):
-        stage, land = ref.stage.at[c], ref.land.at[c]
+    def scatter(c, k, product, hold=False):
+        ref.part[part(k), :] = product
+        ref.stage[c, part(k), :] = product.astype(bf16)
         copies = []
         for o in range(n_mp - 1, 0, -1):
             to = peer_of(o)
-            at = pl.ds(pl.multiple_of(to * own_rows, own_rows), own_rows)
-            stage[at, :] = rows_of(at).astype(bf16)
-            copies.append(message(stage.at[at], land.at[o - 1], (mod, seq, to)))
+            copies.append(message(ref.stage.at[c, share(k, to)], ref.land.at[c, k, o - 1], (mod, seq, to)))
             if not hold:
                 copies[-1].start()
-        ref.keep[c] = rows_of(mine)
+        ref.keep[c, kept(k), :] = ref.part[share(k, mp), :]
         return copies
 
-    def summed(c, copies):
+    def summed(c, k, copies):
         for copy in copies:
             copy.wait_recv()
-        total = ref.keep[c]
+        total = ref.keep[c, kept(k), :]
         for o in range(1, n_mp):
-            total += ref.land[c, o - 1].astype(f32)
+            total += ref.land[c, k, o - 1].astype(f32)
         return total
 
-    def gather(c):
-        whole = ref.whole.at[c]
-        copies = [
-            message(whole.at[mine], whole.at[mine], (mod, seq, peer_of(o))) for o in range(1, n_mp)
-        ]
+    def gather(c, k):
+        at = ref.whole.at[c, share(k, mp)]
+        copies = [message(at, at, (mod, seq, peer_of(o))) for o in range(1, n_mp)]
         for copy in reversed(copies):
             copy.start()
         return copies
 
-    attn_sum = scatter(0, lambda at: nn(ref.att[at, :], ref.wo[...]))
+    loads.wo.wait()
+    attn_sum = []
+    for k in parts:
+        lax.fori_loop(0, heads, functools.partial(head_fwd, k), 0)
+        ref.att[part(k), :] = ref.att_t[:, part(k)].T.astype(bf16)
+        attn_sum.append(scatter(0, k, nn(ref.att[part(k), :], ref.wo[...])))
+    att_sent = message(ref.att, ref.att_r, sibling)
+    att_sent.start()
     loads.wd.wait()
     ref.hg[...] = nt(ref.cot[...], ref.wd[...])
     loads.fg.wait()
     ffn_gain = flat(ref.fg)
-    middle = ref.united[mine, :] + summed(0, attn_sum)
-    ref.mid[...] = middle
-    ref.whole[0, mine, :] = (middle * rms_scale(middle) * ffn_gain).astype(bf16)
-    nf_parts = gather(0)
-
-    def to_inner(who):
-        at = pl.ds(pl.multiple_of(who * own_rows, own_rows), own_rows)
+    nf_end = []
+
+    def to_inner(k, who):
+        at = share(k, who)
         copy = message(ref.whole.at[0, at], ref.nf_e.at[at], inner, is_end)
         when(is_end, copy.start)
-        return copy
-
-    nf_end = [to_inner(mp)]
+        nf_end.append(copy)
+
+    nf_parts = []
+    for k in parts:
+        middle = ref.united[share(k, mp), :] + summed(0, k, attn_sum[k])
+        ref.mid[kept(k), :] = middle
+        ref.whole[0, share(k, mp), :] = (middle * rms_scale(middle) * ffn_gain).astype(bf16)
+        nf_parts.append(gather(0, k))
+        to_inner(k, mp)
     tan_e_sent = message(x_tan_e.s, x_tan_e.r, sibling, is_inner)
 
     @pl.when(is_inner)
@@ -337,11 +351,6 @@
 
     loads.wg.wait()
     loads.wu.wait()
-    for o, copy in enumerate(nf_parts, 1):
-        copy.wait_recv()
-        nf_end.append(to_inner(source_of(o)))
-    ref.gate[...] = nt(ref.whole[0], ref.wg[...])
-    ref.up[...] = nt(ref.whole[0], ref.wu[...])
 
     def gelu_rows(at, back_ref=ref.hg, hid=ref.hid, gg=ref.gg, ug=ref.ug):
         g, u, back = ref.gate[at, :], ref.up[at, :], back_ref[at, :]
@@ -354,8 +363,16 @@
         gg[at, :] = (back * u * slope).astype(bf16)
         ug[at, :] = (back * gelu).astype(bf16)
 
-    row_chunks(rows, 32, gelu_rows)
-    ffn_in = scatter(1, lambda at: nn(ref.gg[at, :], ref.wg[...]) + nn(ref.ug[at, :], ref.wu[...]))
+    ffn_in = []
+    for k in parts:
+        for o, copy in enumerate(nf_parts[k], 1):
+            copy.wait_recv()
+            to_inner(k, source_of(o))
+        at = part(k)
+        ref.gate[at, :] = nt(ref.whole[0, at, :], ref.wg[...])
+        ref.up[at, :] = nt(ref.whole[0, at, :], ref.wu[...])
+        row_chunks(k * part_rows, part_rows, 32, gelu_rows)
+        ffn_in.append(scatter(1, k, nn(ref.gg[at, :], ref.wg[...]) + nn(ref.ug[at, :], ref.wu[...])))
     hid_sent = message(ref.hid, ref.hid_r, sibling, not_end)
     gg_sent = message(ref.gg, ref.gg_r, sibling, not_end)
     ug_sent = message(ref.ug, ref.ug_r, sibling, not_end)
@@ -367,7 +384,7 @@
     after = (mod, jnp.minimum(seq + 1, n_seq - 1), mp)
     before = (mod, jnp.maximum(seq - 1, 0), mp)
     weights = []
-    ends = (1, 1, 1, 0, 0)
+    ends = (1, 1, 1, 0, 0, 0, 0)
     for e, g, s, a, b, o in zip(ends, ref.wgrad, ref.wsend, ref.wleft, ref.wright, ref.wout, strict=True):
         right, left = {}, {}
         for j in range(n_seq):
@@ -377,7 +394,7 @@
             if j < n_seq - 1 - e:
                 left[j] = message(s.at[rng], b.at[rng], before, (seq < n_seq - e) & (seq > j))
         weights.append(types.SimpleNamespace(e=e, g=g, s=s, a=a, b=b, o=o, right=right, left=left))
-    w_down, w_gate, w_up, w_proj, w_qkv = weights
+    w_down, w_gate, w_up, w_proj, w_q, w_k, w_v = weights
 
     def product(w, x, pieces, more=False):
         lo = 0
@@ -389,31 +406,34 @@
             w.g[:, lo : lo + size] = both
             lo += size
 
-    def hop(w, step):
-        if step >= n_seq - 1 - w.e:
+    def hop(group, step, some=slice(None)):
+        edge = group[0].e + step
+        if edge >= n_seq - 1:
             return
 
-        @pl.when(seq == w.e + step)
+        @pl.when(seq == edge)
         def _():
-            for j in range(n_seq - 1, w.e + step, -1):
+            for j in list(range(n_seq - 1, edge, -1))[some]:
                 rng = slice(j * block, (j + 1) * block)
-                value = w.g[rng, :]
-                if step > 0:
-                    w.right[j].wait_recv()
-                    value += w.a[rng, :].astype(f32)
-                w.s[rng, :] = value.astype(bf16)
-                w.right[j].start()
-
-        @pl.when(seq == n_seq - 1 - w.e - step)
+                for w in group:
+                    value = w.g[rng, :]
+                    if step > 0:
+                        w.right[j].wait_recv()
+                        value += w.a[rng, :].astype(f32)
+                    w.s[rng, :] = value.astype(bf16)
+                    w.right[j].start()
+
+        @pl.when(seq == n_seq - 1 - edge)
         def _():
-            for j in range(n_seq - 1 - w.e - step):
+            for j in list(range(n_seq - 1 - edge))[some]:
                 rng = slice(j * block, (j + 1) * block)
-                value = w.g[rng, :]
-                if step > 0:
-                    w.left[j].wait_recv()
-                    value += w.b[rng, :].astype(f32)
-                w.s[rng, :] = value.astype(bf16)
-                w.left[j].start()
+                for w in group:
+                    value = w.g[rng, :]
+                    if step > 0:
+                        w.left[j].wait_recv()
+                        value += w.b[rng, :].astype(f32)
+                    w.s[rng, :] = value.astype(bf16)
+                    w.left[j].start()
 
     def arrive(w):
         for j in range(n_seq):
@@ -430,24 +450,28 @@
                     value += w.b[rng, :].astype(f32)
                 w.o[...] = value
 
+    gain_sums = []
+    branch_parts = []
+
+    def middle_back(k):
+        normed_grad = summed(1, k, ffn_in[k])
+        middle = ref.mid[kept(k), :]
+        scale = rms_scale(middle)
+        spread = normed_grad * ffn_gain
+        gain_sums.append(jnp.sum(normed_grad * middle * scale, axis=0, keepdims=True))
+        middle_grad = (
+            ref.cot[share(k, mp), :].astype(f32)
+            + scale * spread
+            - middle * (scale * scale * scale) * jnp.mean(spread * middle, axis=-1, keepdims=True)
+        )
+        ref.mgrad[kept(k), :] = middle_grad
+        ref.whole[1, share(k, mp), :] = middle_grad.astype(bf16)
+        branch_parts.append(gather(1, k))
+
     hid_e_sent = message(ref.hid_e, ref.hid_er, sibling, is_inner)
     gg_e_sent = message(ref.gg_e, ref.gg_er, sibling, is_inner)
     ug_e_sent = message(ref.ug_e, ref.ug_er, sibling, is_inner)
     nf_e_sent = message(x_nf_e.s, x_nf_e.r, sibling, is_inner)
-
-    @pl.when(is_inner)
-    def _():
-        for copy in nf_end:
-            copy.wait_recv()
-        ref.gate[...] = nt(ref.nf_e[...], ref.wg[...])
-        ref.up[...] = nt(ref.nf_e[...], ref.wu[...])
-        row_chunks(rows, 32, lambda at: gelu_rows(at, ref.hg_e, ref.hid_e, ref.gg_e, ref.ug_e))
-        hid_e_sent.start()
-        x_nf_e.s[...] = ref.nf_e[:, there].T
-        nf_e_sent.start()
-        gg_e_sent.start()
-        ug_e_sent.start()
-        x_nf_e.t[...] = ref.nf_e[:, here].T
 
     @pl.when(not_end)
     def _():
@@ -460,6 +484,24 @@
         ug_sent.wait_recv()
         product(w_up, x_nf, [(ref.ug, ref.ug_r)])
 
+    for k in parts:
+        middle_back(k)
+
+    @pl.when(is_inner)
+    def _():
+        for copy in nf_end:
+            copy.wait_recv()
+        ref.gate[...] = nt(ref.nf_e[...], ref.wg[...])
+        ref.up[...] = nt(ref.nf_e[...], ref.wu[...])
+        row_chunks(0, rows, 32, lambda at: gelu_rows(at, ref.hg_e, ref.hid_e, ref.gg_e, ref.ug_e))
+        hid_e_sent.start()
+        x_nf_e.s[...] = ref.nf_e[:, there].T
+        nf_e_sent.start()
+        gg_e_sent.start()
+        ug_e_sent.start()
+        x_nf_e.t[...] = ref.nf_e[:, here].T
+
+
     def end_products(w, x, pieces, needs):
         @pl.when(is_inner)
         def _():
@@ -467,32 +509,13 @@
                 copy.wait_recv()
             product(w, x, pieces, more=True)
 
-        hop(w, 0)
-
-    normed_grad = summed(1, ffn_in)
-    middle = ref.mid[...]
-    scale = rms_scale(middle)
-    spread = normed_grad * ffn_gain
-    ffn_gain_grad = jnp.sum(normed_grad * middle * scale, axis=0, keepdims=True)
-    middle_grad = (
-        ref.cot[mine, :].astype(f32)
-        + scale * spread
-        - middle * (scale * scale * scale) * jnp.mean(spread * middle, axis=-1, keepdims=True)
-    )
-    ref.mgrad[...] = middle_grad
-    ref.whole[1, mine, :] = middle_grad.astype(bf16)
-    branch_parts = gather(1)
-
+        hop([w], 0, slice(0, 1))
+
+    ffn_out = [scatter(2, k, nn(ref.hid[part(k), :], ref.wd[...]), hold=True) for k in parts]
     end_products(w_down, x_tan_e, [(ref.hid_e, ref.hid_er)], (hid_e_sent, tan_e_sent))
     end_products(w_gate, x_nf_e, [(ref.gg_e, ref.gg_er)], (gg_e_sent, nf_e_sent))
     end_products(w_up, x_nf_e, [(ref.ug_e, ref.ug_er)], (ug_e_sent,))
-    ffn_out = scatter(2, lambda at: nn(ref.hid[at, :], ref.wd[...]), hold=True)
-    for copy in branch_parts:
-        copy.wait_recv()
-    for copy in ffn_out:
-        copy.start()
-    ref.ga[...] = nt(ref.whole[1], ref.wo[...]).astype(bf16)
-    branch_sent = transposed(ref.whole.at[1], x_branch)
+    hop([w_down, w_gate, w_up], 0, slice(1, None))
 
     flip = (
         lax.broadcasted_iota(jnp.int32, (rows, rows), 0) // 64 == lax.broadcasted_iota(jnp.int32, (rows, rows), 1) // 64
@@ -505,63 +528,83 @@
     ref.dk[...] = jnp.zeros((2 * rows, width), f32)
     ref.dv[...] = jnp.zeros((2 * rows, width), f32)
 
-    def head_bwd(h, carry):
-        gm = ref.ga[...] * head_mask(h)
-        p0, p1 = ref.prob[h, :rows, :], ref.prob[h, rows:, :]
+    def head_bwd(k, h, carry):
+        a = part(k)
+        gm = ref.ga[a, :] * head_mask(h)
+        p0, p1 = ref.prob[h, :rows, a], ref.prob[h, rows:, a]
         d0 = nt(ref.kv[:, width:], gm)
         d1 = nt(ref.kvr[:, width:], gm)
-        inner = jnp.sum(p0 * d0, axis=0, keepdims=True) + jnp.sum(p1 * d1, axis=0, keepdims=True)
-        g0 = (p0 * (d0 - inner)).astype(bf16)
-        g1 = (p1 * (d1 - inner)).astype(bf16)
+        inner_sum = jnp.sum(p0 * d0, axis=0, keepdims=True) + jnp.sum(p1 * d1, axis=0, keepdims=True)
+        g0 = (p0 * (d0 - inner_sum)).astype(bf16)
+        g1 = (p1 * (d1 - inner_sum)).astype(bf16)
         keys_t = ref.kvt[head_rows(h), :]
-        ref.dq_t[head_rows(h), :] = nn(keys_t[:, :rows], g0) + nn(keys_t[:, rows:], g1)
-        qm = ref.qm[h]
+        ref.dq_t[head_rows(h), a] = nn(keys_t[:, :rows], g0) + nn(keys_t[:, rows:], g1)
+        qm = ref.qm[h, a, :]
         ref.dk[:rows, :] += nn(g0, qm)
         ref.dk[rows:, :] += nn(g1, qm)
         ref.dv[:rows, :] += nn(p0.astype(bf16), gm)
         ref.dv[rows:, :] += nn(p1.astype(bf16), gm)
         turn = ref.turn[...]
+        low, wide = k * part_rows, part_rows + 128
         for side, g in ((0, g0), (1, g1)):
             turned = nn(turn, g)
             for at in range(blocks):
                 piece = turned[at * 64 : at * 64 + 64, :]
-                piece = jnp.concatenate([piece, jnp.zeros((64, 384 - rows), f32)], axis=1)
+                piece = jnp.concatenate([piece, jnp.zeros((64, 128), f32)], axis=1)
                 piece = pltpu.roll(piece, 1, 1, stride=1, stride_axis=0)
-                ref.diag[side * blocks + at, pl.ds(h, 1), :] = jnp.sum(piece, axis=0, keepdims=True)
+                ref.diag[side * blocks + at, pl.ds(h, 1), low : low + wide] += jnp.sum(piece, axis=0, keepdims=True)
         return carry
 
-    lax.fori_loop(0, heads, head_bwd, 0)
+    ref.diag[...] = jnp.zeros(ref.diag.shape, f32)
+    for k in parts:
+        for copy in branch_parts[k]:
+            copy.wait_recv()
+        ref.ga[part(k), :] = nt(ref.whole[1, part(k), :], ref.wo[...]).astype(bf16)
+        if k == PARTS - 1:
+            for copies in ffn_out:
+                for copy in copies:
+                    copy.start()
+        lax.fori_loop(0, heads, functools.partial(head_bwd, k), 0)
+    branch_sent = transposed(ref.whole.at[1], x_branch)
     ref.kvg_s[:, :width] = (ref.dk[rows:, :] * 0.125).astype(bf16)
     ref.kvg_s[:, width:] = ref.dv[rows:, :].astype(bf16)
     kvg_sent = message(ref.kvg_s, ref.kvg_r, sibling)
     kvg_sent.start()
-    ref.whole[2, mine, :] = (ref.mid[...] + summed(2, ffn_out)).astype(bf16)
-    output_parts = gather(2)
+    ref.dqb[...] = (ref.dq_t[...].T * 0.125).astype(bf16)
+    dq_sent = message(ref.dqb, ref.dq_r, sibling)
+    dq_sent.start()
     att_sent.wait_recv()
     branch_sent.wait_recv()
     product(w_proj, x_branch, [(ref.att, ref.att_r)])
-    hop(w_proj, 0)
-    ref.dqb[...] = (ref.dq_t[...].T * 0.125).astype(bf16)
+    hop([w_proj], 0)
+    hop([w_down, w_gate], 1)
+    na_sent.wait_recv()
+    dq_sent.wait_recv()
+    product(w_q, x_na, [(ref.dqb, ref.dq_r)])
+    hop([w_q], 0)
     kvg_sent.wait_recv()
     ref.dkb[...] = (ref.dk[:rows, :] * 0.125 + ref.kvg_r[:, :width].astype(f32)).astype(bf16)
     ref.dvb[...] = (ref.dv[:rows, :] + ref.kvg_r[:, width:].astype(f32)).astype(bf16)
-
-    def attn_rows(at):
-        rows_in = nt(ref.dqb[at, :], ref.wq[...]) + nt(ref.dkb[at, :], ref.wk[...]) + nt(ref.dvb[at, :], ref.wv[...])
-        ref.part2[at, :] = rows_in
-        return rows_in
-
-    attn_in = scatter(3, attn_rows)
-    dq_sent = message(ref.dqb, ref.dq_r, sibling)
     dk_sent = message(ref.dkb, ref.dk_r, sibling)
     dv_sent = message(ref.dvb, ref.dv_r, sibling)
-    for copy in (dq_sent, dk_sent, dv_sent):
+    for copy in (dk_sent, dv_sent):
         copy.start()
+    attn_in = []
+    for k in parts:
+        at = part(k)
+        rows_in = nt(ref.dqb[at, :], ref.wq[...]) + nt(ref.dkb[at, :], ref.wk[...]) + nt(ref.dvb[at, :], ref.wv[...])
+        attn_in.append(scatter(3, k, rows_in))
+    for copy in (dk_sent, dv_sent):
+        copy.wait_recv()
+    product(w_k, x_na, [(ref.dkb, ref.dk_r)])
+    product(w_v, x_na, [(ref.dvb, ref.dv_r)])
+    hop([w_k, w_v], 0)
+    hop([w_up], 1)
 
     def gain_rows(i, total):
         at = pl.ds(pl.multiple_of(i * 32, 32), 32)
         u = ref.united[at, :]
-        return total + jnp.sum(ref.part2[at, :] * u * rms_scale(u), axis=0, keepdims=True)
+        return total + jnp.sum(ref.part[at, :] * u * rms_scale(u), axis=0, keepdims=True)
 
     attn_gain_grad = lax.fori_loop(0, rows // 32, gain_rows, jnp.zeros((1, dim), f32))
 
@@ -580,7 +623,7 @@
         total[:, :SPANS], ref.hot[...], (((1,), (1,)), ((), ())), precision=lax.Precision.HIGHEST, preferred_element_type=f32
     )
     quarter = dim // 4
-    for i, line in enumerate((attn_gain_grad, ffn_gain_grad)):
+    for i, line in enumerate((attn_gain_grad, sum(gain_sums))):
         for k in range(4):
             ref.small[4 * i + k : 4 * i + k + 1, :quarter] = line[:, k * quarter : (k + 1) * quarter]
     ref.small[:, quarter:] = jnp.zeros((8, 128), f32)
@@ -589,13 +632,7 @@
     for copy in small_mp:
         copy.start()
 
-    for copy in (na_sent, dq_sent, dk_sent, dv_sent):
-        copy.wait_recv()
-    product(w_qkv, x_na, [(ref.dqb, ref.dq_r), (ref.dkb, ref.dk_r), (ref.dvb, ref.dv_r)])
-    hop(w_qkv, 0)
-    hop(w_down, 1)
-    hop(w_proj, 1)
-    hop(w_gate, 1)
+    hop([w_proj, w_q], 1)
     for copy in small_mp:
         copy.wait_recv()
     gains = ref.small[:, :quarter]
@@ -606,17 +643,24 @@
     small_mod = message(ref.small2, ref.small_m, sibling)
     small_mod.start()
 
-    normed_grad = summed(3, attn_in)
-    u = ref.united[mine, :]
-    scale = rms_scale(u)
-    spread = normed_grad * attn_gain
-    united_grad = (
-        ref.mgrad[...]
-        + scale * spread
-        - u * (scale * scale * scale) * jnp.mean(spread * u, axis=-1, keepdims=True)
-    )
-    ref.whole[3, mine, :] = united_grad.astype(bf16)
-    united_parts = gather(3)
+    united_parts = []
+    for k in parts:
+        normed_grad = summed(3, k, attn_in[k])
+        u = ref.united[share(k, mp), :]
+        scale = rms_scale(u)
+        spread = normed_grad * attn_gain
+        united_grad = (
+            ref.mgrad[kept(k), :]
+            + scale * spread
+            - u * (scale * scale * scale) * jnp.mean(spread * u, axis=-1, keepdims=True)
+        )
+        ref.whole[3, share(k, mp), :] = united_grad.astype(bf16)
+        united_parts.append(gather(3, k))
+    output_parts = []
+    for k in parts:
+        ref.whole[2, share(k, mp), :] = (ref.mid[kept(k), :] + summed(2, k, ffn_out[k])).astype(bf16)
+        output_parts.append(gather(2, k))
+    hop([w_k, w_v], 1)
     small_mod.wait_recv()
     ref.small3[...] = ref.small2[...] + ref.small_m[...]
     small_seq = [
@@ -624,27 +668,22 @@
     ]
     for copy in small_seq:
         copy.start()
-    hop(w_up, 1)
-    hop(w_qkv, 1)
+    backs = []
+    for k in parts:
+        for o in range(n_mp):
+            at = share(k, source_of(o) if o else mp)
+            if o:
+                united_parts[k][o - 1].wait_recv()
+            back = message(ref.whole.at[3, at], ref.text_o.at[at], sibling, mod == 1)
+            when(mod == 1, back.start)
+            backs.append(back)
     for step in range(2, n_seq - 1):
-        for w in weights:
-            hop(w, step)
-
-    backs = []
-    for o in range(n_mp):
-        who = mp if o == 0 else source_of(o)
-        at = pl.ds(pl.multiple_of(who * own_rows, own_rows), own_rows)
-        if o:
-            united_parts[o - 1].wait_recv()
-        back = message(ref.whole.at[3, at], ref.text_o.at[at], sibling, mod == 1)
-
-        @pl.when(mod == 1)
-        def _(back=back):
-            back.start()
-
-        backs.append(back)
-    for copy in output_parts:
-        copy.wait_recv()
+        hop([w_down, w_gate, w_up], step)
+        hop([w_proj, w_q], step)
+        hop([w_k, w_v], step)
+    for copies in output_parts:
+        for copy in copies:
+            copy.wait_recv()
     ref.out_o[...] = ref.whole[2]
     ref.own_o[...] = ref.whole[3]
     for w in weights:
@@ -677,7 +716,7 @@
     assert used[0] <= ref.ssem.shape[0]
 
 
-def finish(n_seq, heads, width, ids, valid, own, text, out, gd, gg, gu, go, gqkv, small,
+def finish(n_seq, heads, width, ids, valid, own, text, out, gd, gg, gu, go, gq, gk, gv, small,
            o_out, o_in, o_ag, o_q, o_k, o_v, o_o, o_pb, o_fg, o_gate, o_up, o_down, hold):
     mod, seq = lax.axis_index("mod"), lax.axis_index("seq")
     rows, dim = own.shape
@@ -693,9 +732,9 @@
     def _():
         o_in[0] = own[...].astype(f32)
 
-    o_q[...] = gqkv[:, :width]
-    o_k[...] = gqkv[:, width : 2 * width]
-    o_v[...] = gqkv[:, 2 * width :]
+    o_q[...] = gq[...]
+    o_k[...] = gk[...]
+    o_v[...] = gv[...]
     o_o[...] = go[...].T
     o_gate[...] = gg[...].T
     o_up[...] = gu[...].T
@@ -742,12 +781,12 @@
         wk=((dim, width), bf16), wv=((dim, width), bf16), wo=((width, dim), bf16), wg=((ff, dim), bf16),
         wu=((ff, dim), bf16), wd=((ff, dim), bf16), cot=((rows, dim), bf16), inc=((rows, dim), bf16),
         win=((2 * rows // 64, heads, 384), f32), diag=((2 * rows // 64, heads, 384), f32),
-        bias=((heads, 2 * rows, rows), f32), prob=((heads, 2 * rows, rows), f32), xt=((6, half, rows), bf16), xs=((6, half, rows), bf16), xr=((6, half, rows), bf16),
+        prob=((heads, 2 * rows, rows), f32), xt=((6, half, rows), bf16), xs=((6, half, rows), bf16), xr=((6, half, rows), bf16),
         united=((rows, dim), f32), na=((rows, dim), bf16),
         kv=((rows, 2 * width), bf16), kvr=((rows, 2 * width), bf16), kvt=((2 * width, 2 * rows), bf16),
         q=((rows, width), bf16), qm=((heads, rows, width), bf16), att_t=((width, rows), f32), att=((rows, width), bf16),
-        att_r=((rows, width), bf16), part2=((rows, dim), f32), stage=((4, rows, dim), bf16),
-        land=((4, n_mp - 1, own_rows, dim), bf16), keep=((4, own_rows, dim), f32), whole=((4, rows, dim), bf16),
+        att_r=((rows, width), bf16), part=((rows, dim), f32), stage=((4, rows, dim), bf16),
+        land=((4, PARTS, n_mp - 1, own_rows // PARTS, dim), bf16), keep=((4, own_rows, dim), f32), whole=((4, rows, dim), bf16),
         cot_e=((rows, dim), bf16), nf_e=((rows, dim), bf16), hg_e=((rows, ff), f32), hid_e=((rows, ff), bf16),
         hid_er=((rows, ff), bf16), gg_e=((rows, ff), bf16), gg_er=((rows, ff), bf16), ug_e=((rows, ff), bf16),
         ug_er=((rows, ff), bf16), hg=((rows, ff), f32), mid=((own_rows, dim), f32), mgrad=((own_rows, dim), f32), gate=((rows, ff), f32),
@@ -763,7 +802,7 @@
         small3=small, small_m=small, small_q=((n_seq - 1,) + small[0], f32),
         small_p=((n_mp - 1,) + small[0], f32),
     )
-    count = 40 + 9 * n_mp + 10 * n_seq
+    count = 60 + 20 * n_mp + 14 * n_seq
     order = [(name, 0) for name in given]
     out_shape, scratch = [], []
     for specs, into, make in ((results, out_shape, jax.ShapeDtypeStruct), (held, scratch, pltpu.VMEM)):
@@ -787,7 +826,6 @@
         name="layer",
     )(*given.values())
     *wout, out, own, text, small_sum = done
-    down_sum, gate_sum, up_sum, proj_sum, qkv_sum = wout
     part = dim // (2 * n_seq)
     few = NB // (2 * n_seq)
     shapes = [
@@ -798,13 +836,13 @@
     outs = pl.pallas_call(
         functools.partial(finish, n_seq, heads, width),
         out_shape=[jax.ShapeDtypeStruct(*spec) for spec in shapes],
-        in_specs=[vmem] * 11,
+        in_specs=[vmem] * 13,
         out_specs=[vmem] * 12,
         scratch_shapes=[pltpu.VMEM((128, 8), f32)],
         compiler_params=pltpu.CompilerParams(vmem_limit_bytes=63 * 2**20),
         name="finish",
     )(
-        text_patches, patch_valid, own, text, out, down_sum, gate_sum, up_sum, proj_sum, qkv_sum, small_sum
+        text_patches, patch_valid, own, text, out, *wout, small_sum
     )
     outs = list(outs)
     for i in (9, 10):

time: 97.1 us -> 90.7 us (0.934)
  Pallas kernels: 94.8 us -> 88.4 us
    pallas_call x1, Pallas kernels: 90.9 us -> 84.5 us  [per_device(): pl.pallas_call(functools.partial(mega, n_seq, n_mp, heads, order), out_sh...]
where the time goes in v3:
time: 90.7 us; the launch traced here: 90.5 us
  Pallas kernels  88.4 us (97%)
  local copies, waits for them, and re-layouts  1.28 us (1%)
    pallas_call x1, Pallas kernels, per_device(): pl.pallas_call(functools.partial(mega, n_seq, n_mp, heads, order), out_sh...  84.5 us
    pallas_call x1, Pallas kernels, per_device(): pl.pallas_call(functools.partial(finish, n_seq, heads, width), out_shape=...  3.96 us

profile of v3, /device:TPU:0, one launch (start us, length us, event | category | flops | bytes accessed | tf_op | source)
XLA Modules:
  0.0 90.5 jit_solution(7377346678916708754)
XLA Ops:
  0.6 1.3 %pad_bitcast_fusion.refs_4_ = s32[5,128]{1,0:T(8,128)} fusion(s32[639]{0:T(1024)} %param.20), kind=kLoop, calls=%fused_computation | loop fusion | bytes 5116 | tf_op jit(solution)/shard_map/reshape | solution.py:765
  1.9 84.5 %layer.1 = (f32[128,704]{1,0:T(8,128)}, f32[128,704]{1,0:T(8,128)}, f32[128,704]{1,0:T(8,128)}, f32[128,256]{1,0:T(8,128)}, f32[128,256]{1,0:T(8,128)}, /*index=...) custom-call(s32[1,2]{1,0:T(1,128)} %refs_0_.1, ...), custom_call_target="tpu_custom_call" | custom-call | tf_op jit(solution)/shard_map/layer/pallas_call | solution.py:817
  86.4 4.0 %finish.1 = (bf16[1,256,1024]{2,1,0:T(8,128)(2,1)}, f32[1,256,1024]{2,1,0:T(8,128)}, f32[1,128]{1,0:T(1,128)}, f32[128,256]{1,0:T(8,128)}, f32[128,256]{1,0:T(8,...) custom-call(s32[4,256]{1,0:T(4,128)} %bitcast.16, ...), custom_call_target="tpu_custom_call" | custom-call | tf_op jit(solution)/shard_map/finish/pallas_call | solution.py:836

commit v4 on v3

--- a/solution.py
+++ b/solution.py
@@ -129,14 +129,14 @@
 
     loads = types.SimpleNamespace()
     pairs = (
-        (ref.inp_h.at[0], ref.inp), (ref.ids_h, ref.ids), (ref.pb_h, ref.pb), (ref.tp_h, ref.tp), (ref.pv_h, ref.pv),
+        (ref.inp_h.at[0], ref.inp), (ref.pb_h, ref.pb), (ref.tp_h, ref.tp), (ref.pv_h, ref.pv),
         (ref.ag_h, ref.ag), (ref.wk_h, ref.wk), (ref.wv_h, ref.wv), (ref.wq_h, ref.wq), (ref.cot_h.at[0], ref.cot),
         (ref.wo_h, ref.wo), (ref.wd_h, ref.wd), (ref.fg_h, ref.fg), (ref.wg_h, ref.wg), (ref.wu_h, ref.wu),
     )
     copies = [pltpu.make_async_copy(src, dst, ref.lsem.at[i]) for i, (src, dst) in enumerate(pairs)]
     for copy in copies:
         copy.start()
-    (loads.inp, loads.ids, loads.pb, loads.tp, loads.pv, loads.ag, loads.wk, loads.wv, loads.wq, loads.cot, loads.wo,
+    (loads.inp, loads.pb, loads.tp, loads.pv, loads.ag, loads.wk, loads.wv, loads.wq, loads.cot, loads.wo,
      loads.wd, loads.fg, loads.wg, loads.wu) = copies
 
     barrier = pltpu.get_barrier_semaphore()
@@ -159,13 +159,22 @@
 
     first = ref.len_s[0, 0]
     long_first = first == LONG
-    loads.ids.wait()
     loads.pb.wait()
     mirror = (
         lax.broadcasted_iota(jnp.int32, (128, 128), 0) + lax.broadcasted_iota(jnp.int32, (128, 128), 1) == 127
     ).astype(f32)
-    turned_ids = nn(ref.ids[...].astype(f32).astype(bf16), mirror.astype(bf16))
-    lines = turned_ids.shape[0]
+    places = lax.broadcasted_iota(jnp.int32, (8, 128), 0) * 128 + lax.broadcasted_iota(jnp.int32, (8, 128), 1)
+    span = ref.ids_s.shape[0]
+    stride = 9 if span % 9 == 0 else 1
+
+    def set_ids(i, ids):
+        for k in range(stride):
+            ids = jnp.where(places == i * stride + k, ref.ids_s[i * stride + k], ids)
+        return ids
+
+    ids = lax.fori_loop(0, span // stride, set_ids, jnp.zeros((8, 128), jnp.int32))
+    turned_ids = nn(ids.astype(f32).astype(bf16), mirror.astype(bf16))
+    lines = SPANS // 128
     turned_ids = jnp.concatenate([turned_ids[i : i + 1, :] for i in reversed(range(lines))], axis=1)
     hot = bucket_hot(turned_ids.astype(jnp.int32))
     ref.hot[...] = hot
@@ -484,9 +493,7 @@
         ug_sent.wait_recv()
         product(w_up, x_nf, [(ref.ug, ref.ug_r)])
 
-    for k in parts:
-        middle_back(k)
-
+    middle_back(0)
     @pl.when(is_inner)
     def _():
         for copy in nf_end:
@@ -502,6 +509,9 @@
         x_nf_e.t[...] = ref.nf_e[:, here].T
 
 
+    for k in parts[1:]:
+        middle_back(k)
+
     def end_products(w, x, pieces, needs):
         @pl.when(is_inner)
         def _():
@@ -511,11 +521,11 @@
 
         hop([w], 0, slice(0, 1))
 
-    ffn_out = [scatter(2, k, nn(ref.hid[part(k), :], ref.wd[...]), hold=True) for k in parts]
     end_products(w_down, x_tan_e, [(ref.hid_e, ref.hid_er)], (hid_e_sent, tan_e_sent))
     end_products(w_gate, x_nf_e, [(ref.gg_e, ref.gg_er)], (gg_e_sent, nf_e_sent))
     end_products(w_up, x_nf_e, [(ref.ug_e, ref.ug_er)], (ug_e_sent,))
     hop([w_down, w_gate, w_up], 0, slice(1, None))
+    ffn_out = [scatter(2, k, nn(ref.hid[part(k), :], ref.wd[...]), hold=True) for k in parts]
 
     flip = (
         lax.broadcasted_iota(jnp.int32, (rows, rows), 0) // 64 == lax.broadcasted_iota(jnp.int32, (rows, rows), 1) // 64
@@ -762,9 +772,8 @@
     block = half // n_seq
     text_patches, patch_valid, position_bias = text_patches.T, patch_valid.T, position_bias.T
     gate_weight, up_weight = gate_weight.T, up_weight.T
-    ids = jnp.pad(bucket_table, (0, SPANS - bucket_table.shape[0])).reshape(SPANS // 128, 128)
     given = dict(
-        len_s=text_lengths, inp_h=inputs, tp_h=text_patches, pv_h=patch_valid, ids_h=ids, pb_h=position_bias,
+        len_s=text_lengths, ids_s=bucket_table, inp_h=inputs, tp_h=text_patches, pv_h=patch_valid, pb_h=position_bias,
         ag_h=attn_gain.reshape(dim // 128, 128), fg_h=ffn_gain.reshape(dim // 128, 128), wq_h=query_weight, wk_h=key_weight,
         wv_h=value_weight, wo_h=output_weight, wg_h=gate_weight, wu_h=up_weight, wd_h=down_weight, cot_h=cotangent,
     )
@@ -776,7 +785,7 @@
     small = ((8, dim // 4 + 128), f32)
     sent = [((half, size), bf16) for size in sizes]
     held = dict(
-        inp=((rows, dim), bf16), ids=(ids.shape, jnp.int32), hot=((NB, SPANS), f32), pb=((heads, NB), f32), tp=(text_patches.shape, jnp.int32),
+        inp=((rows, dim), bf16), hot=((NB, SPANS), f32), pb=((heads, NB), f32), tp=(text_patches.shape, jnp.int32),
         pv=(patch_valid.shape, jnp.int32), ag=((dim // 128, 128), bf16), fg=((dim // 128, 128), bf16), wq=((dim, width), bf16),
         wk=((dim, width), bf16), wv=((dim, width), bf16), wo=((width, dim), bf16), wg=((ff, dim), bf16),
         wu=((ff, dim), bf16), wd=((ff, dim), bf16), cot=((rows, dim), bf16), inc=((rows, dim), bf16),
@@ -805,26 +814,26 @@
     count = 60 + 20 * n_mp + 14 * n_seq
     order = [(name, 0) for name in given]
     out_shape, scratch = [], []
-    for specs, into, make in ((results, out_shape, jax.ShapeDtypeStruct), (held, scratch, pltpu.VMEM)):
+    for specs, into, make in ((results, out_shape, pltpu.VMEM), (held, scratch, pltpu.VMEM)):
         for name, spec in specs.items():
             many = spec if isinstance(spec, list) else [spec]
             order.append((name, len(many) if isinstance(spec, list) else 0))
             into.extend(make(*one) for one in many)
-    for i, size in enumerate((count, count, len(given) - 1)):
+    for i, size in enumerate((count, count, len(given) - 2)):
         order.append((("ssem", "rsem", "lsem")[i], 0))
         scratch.append(pltpu.SemaphoreType.DMA((size,)))
     vmem = pl.BlockSpec(memory_space=pltpu.VMEM)
     done = pl.pallas_call(
         functools.partial(mega, n_seq, n_mp, heads, order),
         out_shape=out_shape,
-        in_specs=[pl.BlockSpec(memory_space=pltpu.SMEM)] + [pl.BlockSpec(memory_space=pl.ANY)] * (len(given) - 1),
-        out_specs=[vmem] * len(out_shape),
+        in_specs=[pl.BlockSpec(memory_space=pltpu.SMEM)] * 2 + [pl.BlockSpec(memory_space=pl.ANY)] * (len(given) - 2),
         scratch_shapes=scratch,
         compiler_params=pltpu.CompilerParams(
-            collective_id=0, has_side_effects=True, vmem_limit_bytes=63 * 2**20
+            collective_id=0, has_side_effects=True, vmem_limit_bytes=58 * 2**20
         ),
         name="layer",
     )(*given.values())
+    done = [pltpu.with_memory_space_constraint(one, pltpu.VMEM) for one in done]
     *wout, out, own, text, small_sum = done
     part = dim // (2 * n_seq)
     few = NB // (2 * n_seq)
@@ -839,7 +848,7 @@
         in_specs=[vmem] * 13,
         out_specs=[vmem] * 12,
         scratch_shapes=[pltpu.VMEM((128, 8), f32)],
-        compiler_params=pltpu.CompilerParams(vmem_limit_bytes=63 * 2**20),
+        compiler_params=pltpu.CompilerParams(vmem_limit_bytes=16 * 2**20),
         name="finish",
     )(
         text_patches, patch_valid, own, text, out, *wout, small_sum

time: 90.7 us -> 85.4 us (0.942)
  Pallas kernels: 88.4 us -> 84.5 us
  local copies, waits for them, and re-layouts: 1.28 us -> 0.01 us
    pallas_call x1, Pallas kernels: 84.5 us -> 82.1 us  [per_device(): pl.pallas_call(functools.partial(mega, n_seq, n_mp, heads, order), out_sh...]
    pallas_call x1, Pallas kernels: 3.96 us -> 2.42 us  [per_device(): pl.pallas_call(functools.partial(finish, n_seq, heads, width), out_shape=...]
    reshape x1 -> x0, local copies, waits for them, and re-layouts: 1.28 us -> none  [per_device(): jnp.pad(bucket_table, (0, SPANS - bucket_table.shape[0]))]
where the time goes in v4:
time: 85.4 us; the launch traced here: 85.2 us
  Pallas kernels  84.5 us (99%)
    pallas_call x1, Pallas kernels, per_device(): pl.pallas_call(functools.partial(mega, n_seq, n_mp, heads, order), out_sh...  82.1 us
    pallas_call x1, Pallas kernels, per_device(): pl.pallas_call(functools.partial(finish, n_seq, heads, width), out_shape=...  2.42 us

profile of v4, /device:TPU:0, one launch (start us, length us, event | category | flops | bytes accessed | tf_op | source)
XLA Modules:
  0.0 85.2 jit_solution(15948165522757684096)
XLA Ops:
  0.7 0.0 copy-start
  0.7 0.0 copy-start.1
  0.7 82.1 %layer.1 = (f32[128,704]{1,0:T(8,128)S(1)}, f32[128,704]{1,0:T(8,128)S(1)}, f32[128,704]{1,0:T(8,128)S(1)}, f32[128,256]{1,0:T(8,128)S(1)}, f32[128,256]{1,0:T(8...) custom-call(s32[1,2]{1,0:T(1,128)} %refs_0_.1, ...), custom_call_target="tpu_custom_call" | custom-call | tf_op jit(solution)/shard_map/layer/pallas_call | solution.py:826
  82.7 0.0 copy-done
  82.8 0.0 copy-done.1
  82.8 2.4 %finish.1 = (bf16[1,256,1024]{2,1,0:T(8,128)(2,1)}, f32[1,256,1024]{2,1,0:T(8,128)}, f32[1,128]{1,0:T(1,128)}, f32[128,256]{1,0:T(8,128)}, f32[128,256]{1,0:T(8,...) custom-call(s32[4,256]{1,0:T(4,128)S(1)} %bitcast.12, ...), custom_call_target="tpu_custom_call" | custom-call | tf_op jit(solution)/shard_map/finish/pallas_call | solution.py:845
Async XLA Ops:
  0.7 82.1 %copy-start = (s32[256,4]{0,1:T(4,128)S(1)}, s32[256,4]{0,1:T(4,128)}, u32[]{:S(2)}) copy-start(s32[256,4]{0,1:T(4,128)} %param.17) | copy-start | bytes 12292
  0.7 82.1 %copy-start.1 = (s32[256,4]{0,1:T(4,128)S(1)}, s32[256,4]{0,1:T(4,128)}, u32[]{:S(2)}) copy-start(s32[256,4]{0,1:T(4,128)} %param.18) | copy-start | bytes 12292

commit v5 on v4

--- a/solution.py
+++ b/solution.py
@@ -575,11 +575,11 @@
                 for copy in copies:
                     copy.start()
         lax.fori_loop(0, heads, functools.partial(head_bwd, k), 0)
-    branch_sent = transposed(ref.whole.at[1], x_branch)
     ref.kvg_s[:, :width] = (ref.dk[rows:, :] * 0.125).astype(bf16)
     ref.kvg_s[:, width:] = ref.dv[rows:, :].astype(bf16)
     kvg_sent = message(ref.kvg_s, ref.kvg_r, sibling)
     kvg_sent.start()
+    branch_sent = transposed(ref.whole.at[1], x_branch)
     ref.dqb[...] = (ref.dq_t[...].T * 0.125).astype(bf16)
     dq_sent = message(ref.dqb, ref.dq_r, sibling)
     dq_sent.start()

time: 85.4 us -> 85.4 us (level)
  no operation moved by 1% of the time
where the time goes in v5:
time: 85.4 us; the launch traced here: 85.2 us
  Pallas kernels  84.5 us (99%)
    pallas_call x1, Pallas kernels, per_device(): pl.pallas_call(functools.partial(mega, n_seq, n_mp, heads, order), out_sh...  82.1 us
    pallas_call x1, Pallas kernels, per_device(): pl.pallas_call(functools.partial(finish, n_seq, heads, width), out_shape=...  2.42 us

profile of v5, /device:TPU:0, one launch (start us, length us, event | category | flops | bytes accessed | tf_op | source)
XLA Modules:
  0.0 85.2 jit_solution(17877669886370616993)
XLA Ops:
  0.7 0.0 copy-start
  0.7 0.0 copy-start.1
  0.7 82.1 %layer.1 = (f32[128,704]{1,0:T(8,128)S(1)}, f32[128,704]{1,0:T(8,128)S(1)}, f32[128,704]{1,0:T(8,128)S(1)}, f32[128,256]{1,0:T(8,128)S(1)}, f32[128,256]{1,0:T(8...) custom-call(s32[1,2]{1,0:T(1,128)} %refs_0_.1, ...), custom_call_target="tpu_custom_call" | custom-call | tf_op jit(solution)/shard_map/layer/pallas_call | solution.py:826
  82.7 0.0 copy-done
  82.8 0.0 copy-done.1
  82.8 2.4 %finish.1 = (bf16[1,256,1024]{2,1,0:T(8,128)(2,1)}, f32[1,256,1024]{2,1,0:T(8,128)}, f32[1,128]{1,0:T(1,128)}, f32[128,256]{1,0:T(8,128)}, f32[128,256]{1,0:T(8,...) custom-call(s32[4,256]{1,0:T(4,128)S(1)} %bitcast.12, ...), custom_call_target="tpu_custom_call" | custom-call | tf_op jit(solution)/shard_map/finish/pallas_call | solution.py:845
Async XLA Ops:
  0.7 82.1 %copy-start = (s32[256,4]{0,1:T(4,128)S(1)}, s32[256,4]{0,1:T(4,128)}, u32[]{:S(2)}) copy-start(s32[256,4]{0,1:T(4,128)} %param.17) | copy-start | bytes 12292
  0.7 82.1 %copy-start.1 = (s32[256,4]{0,1:T(4,128)S(1)}, s32[256,4]{0,1:T(4,128)}, u32[]{:S(2)}) copy-start(s32[256,4]{0,1:T(4,128)} %param.18) | copy-start | bytes 12292

commit v6 on v5

--- a/solution.py
+++ b/solution.py
@@ -380,7 +380,7 @@
         at = part(k)
         ref.gate[at, :] = nt(ref.whole[0, at, :], ref.wg[...])
         ref.up[at, :] = nt(ref.whole[0, at, :], ref.wu[...])
-        row_chunks(k * part_rows, part_rows, 32, gelu_rows)
+        row_chunks(k * part_rows, part_rows, 16, gelu_rows)
         ffn_in.append(scatter(1, k, nn(ref.gg[at, :], ref.wg[...]) + nn(ref.ug[at, :], ref.wu[...])))
     hid_sent = message(ref.hid, ref.hid_r, sibling, not_end)
     gg_sent = message(ref.gg, ref.gg_r, sibling, not_end)
@@ -500,7 +500,7 @@
             copy.wait_recv()
         ref.gate[...] = nt(ref.nf_e[...], ref.wg[...])
         ref.up[...] = nt(ref.nf_e[...], ref.wu[...])
-        row_chunks(0, rows, 32, lambda at: gelu_rows(at, ref.hg_e, ref.hid_e, ref.gg_e, ref.ug_e))
+        row_chunks(0, rows, 16, lambda at: gelu_rows(at, ref.hg_e, ref.hid_e, ref.gg_e, ref.ug_e))
         hid_e_sent.start()
         x_nf_e.s[...] = ref.nf_e[:, there].T
         nf_e_sent.start()

time: 85.4 us -> 85.4 us (level)
  no operation moved by 1% of the time
where the time goes in v6:
time: 85.4 us; the launch traced here: 85.3 us
  Pallas kernels  84.5 us (99%)
    pallas_call x1, Pallas kernels, per_device(): pl.pallas_call(functools.partial(mega, n_seq, n_mp, heads, order), out_sh...  82.1 us
    pallas_call x1, Pallas kernels, per_device(): pl.pallas_call(functools.partial(finish, n_seq, heads, width), out_shape=...  2.42 us

profile of v6, /device:TPU:0, one launch (start us, length us, event | category | flops | bytes accessed | tf_op | source)
XLA Modules:
  0.0 85.3 jit_solution(11059747261922038196)
XLA Ops:
  0.7 0.0 copy-start
  0.7 0.0 copy-start.1
  0.7 82.1 %layer.1 = (f32[128,704]{1,0:T(8,128)S(1)}, f32[128,704]{1,0:T(8,128)S(1)}, f32[128,704]{1,0:T(8,128)S(1)}, f32[128,256]{1,0:T(8,128)S(1)}, f32[128,256]{1,0:T(8...) custom-call(s32[1,2]{1,0:T(1,128)} %refs_0_.1, ...), custom_call_target="tpu_custom_call" | custom-call | tf_op jit(solution)/shard_map/layer/pallas_call | solution.py:826
  82.8 0.0 copy-done
  82.8 0.0 copy-done.1
  82.8 2.4 %finish.1 = (bf16[1,256,1024]{2,1,0:T(8,128)(2,1)}, f32[1,256,1024]{2,1,0:T(8,128)}, f32[1,128]{1,0:T(1,128)}, f32[128,256]{1,0:T(8,128)}, f32[128,256]{1,0:T(8,...) custom-call(s32[4,256]{1,0:T(4,128)S(1)} %bitcast.12, ...), custom_call_target="tpu_custom_call" | custom-call | tf_op jit(solution)/shard_map/finish/pallas_call | solution.py:845
Async XLA Ops:
  0.7 82.1 %copy-start = (s32[256,4]{0,1:T(4,128)S(1)}, s32[256,4]{0,1:T(4,128)}, u32[]{:S(2)}) copy-start(s32[256,4]{0,1:T(4,128)} %param.17) | copy-start | bytes 12292
  0.7 82.1 %copy-start.1 = (s32[256,4]{0,1:T(4,128)S(1)}, s32[256,4]{0,1:T(4,128)}, u32[]{:S(2)}) copy-start(s32[256,4]{0,1:T(4,128)} %param.18) | copy-start | bytes 12292
